TPU v7x, 32 devices: a whole 2x2x4 slice. The times are simulated.
32 devices in a mesh: px: 4 (over y, core), py: 4 (over z), lev: 2 (over x).
Axes of the slice: x: 2, y: 2, z: 4, core: 2. Of those that a mesh axis runs over, the one named last changes fastest.
Arguments:
- tracer: float32 [2, 8, 32, 512], P('lev', None, 'px', 'py'), may hold values from -6 to 6
- node_mass: float32 [2, 32, 512], P('lev', 'px', 'py'), may hold values from 0.5 to 2
- wind_x: float32 [2, 32, 512], P('lev', 'px', 'py'), may hold values from -4 to 4
- wind_y: float32 [2, 32, 512], P('lev', 'px', 'py'), may hold values from -4 to 4
- remap: float32 [2, 2], replicated, may hold values from -4 to 4
Outputs:
- remapped: float32 [2, 8, 32, 512], P(None, 'lev', 'px', 'py')
All inputs are finite; a program needn't handle non-finite values.
Results may differ from a plain program's by a relative error of at most 0.0001.
Values sent between devices are 32-bit elements; how exact they have to be, the bound alone decides.
A program may use at most 64 MiB of HBM per device.

v0:
```python
import jax
import jax.numpy as jnp
import numpy as np
from jax import lax
from jax.sharding import PartitionSpec as P

GLL_NODES = 4


sentinel = 1e30
step_size = 0.1
section_weights = ((0.0, 1.0), (0.75, 0.25), (1.0 / 3.0, 2.0 / 3.0))


def extended(block, sides, width):
    for axis, dim in sides:
        count = lax.axis_size(axis)
        forward = [(i, i + 1) for i in range(count - 1)]
        forward.append((count - 1, 0))
        backward = [(target, source) for source, target in forward]
        low = lax.ppermute(
            lax.slice_in_dim(block, block.shape[dim] - width, None, axis=dim), axis, forward
        )
        high = lax.ppermute(lax.slice_in_dim(block, 0, width, axis=dim), axis, backward)
        block = jnp.concatenate([low, block, high], axis=dim)
    return block


def derivative_table():
    points = np.array([-1.0, -(5.0 ** (-0.5)), 5.0 ** (-0.5), 1.0])
    number = points.shape[0]
    barycentric = np.array(
        [
            1.0
            / np.prod([points[outer] - points[inner] for inner in range(number) if inner != outer])
            for outer in range(number)
        ]
    )
    table = np.zeros((number, number))
    for outer in range(number):
        for inner in range(number):
            if inner != outer:
                table[outer, inner] = (
                    barycentric[inner] / barycentric[outer] / (points[outer] - points[inner])
                )
    for outer in range(number):
        table[outer, outer] = -np.sum(table[outer])
    return table


def block_table(elements):
    return jnp.asarray(np.kron(np.eye(elements), derivative_table()), jnp.float32)


def pair_sum(values, which_axis):
    layout = values.shape
    where_at = len(layout) + which_axis
    elements = layout[where_at] // GLL_NODES
    blocked = values.reshape(layout[:where_at] + (elements, GLL_NODES) + layout[where_at + 1 :])
    head_nodes = lax.slice_in_dim(blocked, 0, 1, axis=where_at + 1)
    tail_nodes = lax.slice_in_dim(blocked, GLL_NODES - 1, GLL_NODES, axis=where_at + 1)
    middle = lax.slice_in_dim(blocked, 1, GLL_NODES - 1, axis=where_at + 1)
    zero_slab = jnp.zeros_like(lax.slice_in_dim(tail_nodes, 0, 1, axis=where_at))
    before = jnp.concatenate(
        [zero_slab, lax.slice_in_dim(tail_nodes, 0, elements - 1, axis=where_at)], axis=where_at
    )
    following = jnp.concatenate(
        [lax.slice_in_dim(head_nodes, 1, elements, axis=where_at), zero_slab], axis=where_at
    )
    joined = jnp.concatenate(
        [head_nodes + before, middle, tail_nodes + following], axis=where_at + 1
    )
    return joined.reshape(layout)


def shared_ext(values, width, keep_rim):
    filler = (GLL_NODES - width % GLL_NODES) % GLL_NODES
    padded = jnp.pad(values, [(0, 0)] * (values.ndim - 2) + [(filler, filler), (filler, filler)])
    summed = pair_sum(pair_sum(padded, -2), -1)
    margin = filler + width - keep_rim
    return summed[..., margin : summed.shape[-2] - margin, margin : summed.shape[-1] - margin]


def edge_cut(values, width, fill_value):
    columns = lax.broadcasted_iota(jnp.int32, values.shape, values.ndim - 1)
    position = lax.axis_index("py")
    cut_mask = (columns < width) & (position == 0) | (columns >= values.shape[-1] - width) & (
        position == lax.axis_size("py") - 1
    )
    return jnp.where(cut_mask, fill_value, values)


def element_extrema(field):
    layout = field.shape
    blocked = field.reshape(
        layout[0], layout[1], layout[2] // GLL_NODES, GLL_NODES, layout[3] // GLL_NODES, GLL_NODES
    )
    return jnp.stack([jnp.min(blocked, axis=(3, 5)), -jnp.max(blocked, axis=(3, 5))])


def bounded(padded):
    rows_min = jnp.minimum(
        jnp.minimum(padded[..., :-2, :], padded[..., 1:-1, :]), padded[..., 2:, :]
    )
    result = jnp.minimum(jnp.minimum(rows_min[..., :-2], rows_min[..., 1:-1]), rows_min[..., 2:])
    return (result[0], -result[1])


def tendency(field, wind_x, wind_y, table_x, table_y):
    slope_x = jnp.einsum(
        "ij,lcjy->lciy", table_x, wind_x[:, None] * field, precision=lax.Precision.HIGHEST
    )
    slope_y = jnp.einsum(
        "lcxj,ij->lcxi", wind_y[:, None] * field, table_y, precision=lax.Precision.HIGHEST
    )
    return field - step_size * (slope_x + slope_y)


def limit(moved, lower, upper):
    layout = moved.shape
    blocked = moved.reshape(
        layout[0], layout[1], layout[2] // GLL_NODES, GLL_NODES, layout[3] // GLL_NODES, GLL_NODES
    )
    clipped = jnp.clip(blocked, lower[:, :, :, None, :, None], upper[:, :, :, None, :, None])
    return clipped.reshape(layout)


def shards(tracer, node_mass, wind_x, wind_y, remap):
    table_x = block_table(tracer.shape[2] // GLL_NODES)
    table_y = block_table(tracer.shape[3] // GLL_NODES)
    rim_width = 1
    keep_rim = 0
    mass_ext = extended(node_mass, (("px", 1), ("py", 2)), rim_width)
    mass_sum = shared_ext(edge_cut(mass_ext, rim_width, 0.0), rim_width, keep_rim)
    mass_sum = edge_cut(mass_sum, keep_rim, 1.0)
    field = tracer
    for share_start, share_new in section_weights:
        extrema = extended(element_extrema(field), (("px", 3), ("py", 4)), 1)
        lower, upper = bounded(edge_cut(extrema, 1, sentinel))
        limited = limit(tendency(field, wind_x, wind_y, table_x, table_y), lower, upper)
        weighted = node_mass[:, None] * limited
        weighted_ext = extended(weighted, (("px", 2), ("py", 3)), 1)
        summed = shared_ext(edge_cut(weighted_ext, 1, 0.0), 1, 0)
        field = share_start * tracer + share_new * (summed / mass_sum[:, None])
    return jnp.einsum(
        "ab,bcxy->acxy",
        remap,
        lax.all_to_all(field, "lev", split_axis=1, concat_axis=0, tiled=True),
        precision=lax.Precision.HIGHEST,
    )


def solution(mesh):
    in_specs = (
        P("lev", None, "px", "py"),
        P("lev", "px", "py"),
        P("lev", "px", "py"),
        P("lev", "px", "py"),
        P(),
    )
    out_specs = P(None, "lev", "px", "py")
    return jax.shard_map(shards, mesh=mesh, in_specs=in_specs, out_specs=out_specs, check_vma=False)
```

profile of v0, /device:TPU:0, one launch (start us, length us, event | category | flops | bytes accessed | tf_op | source)
XLA Modules:
  0.0 88.7 jit_solution(642264675095039472)
XLA Ops:
  0.0 0.8 fusion.66
  0.8 0.5 collective-permute-start.8
  1.3 2.0 %collective-permute-start.9 = (f32[1,1,128]{2,1,0:T(1,128)S(1)}, f32[1,1,128]{2,1,0:T(1,128)S(1)}, u32[]{:S(2)}, u32[]{:S(2)}) collective-permute-start(f32[1,1,128]{2,1,0:T(1,128)S(1)} %get-tuple-element.76), channel_id=1, source_target_pairs={{8,0},{16,8},{24,16},{0,24},{9,1},{17,9},{25,17},{1,25},{10,2},{18... | collective-permute-start | bytes 1544 | tf_op jit(solution)/shard_map/ppermute | solution.py:24
  3.2 1.0 %copy.217 = f32[1,8,8,128]{1,3,2,0:T(8,128)S(1)} copy(f32[1,8,8,128]{3,2,1,0:T(8,128)} %param.7) | data formatting | bytes 65536 | tf_op args[0]
  4.2 0.3 fusion.47
  4.7 0.7 collective-permute-start
  5.3 1.1 %collective-permute-start.1 = (f32[2,1,8,1,32]{4,2,3,1,0:T(8,128)S(1)}, f32[2,1,8,1,32]{4,2,3,1,0:T(8,128)S(1)}, u32[]{:S(2)}, u32[]{:S(2)}) collective-permute-start(f32[2,1,8,1,32]{4,2,3,1,0:T(8,128)S(1)} %get-tuple-element.72), channel_id=1, source_target_pairs={{8,0},{16,8},{24,16},{0,24},{9,1},{17,9},{25,17},{1,25},{10,2},{18... | collective-permute-start | bytes 6152 | tf_op jit(solution)/shard_map/ppermute | solution.py:24
  6.8 2.4 %collective-permute-start.10 = (f32[1,10,1]{2,1,0:T(8,128)S(1)}, f32[1,10,1]{2,1,0:T(8,128)S(1)}, u32[]{:S(2)}, u32[]{:S(2)}) collective-permute-start(f32[1,10,1]{2,1,0:T(8,128)S(1)} %get-tuple-element.73), channel_id=1, source_target_pairs={{0,2},{2,4},{4,6},{6,0},{1,3},{3,5},{5,7},{7,1},{8,10},{10,12},{12... | collective-permute-start | bytes 128 | tf_op jit(solution)/shard_map/ppermute | solution.py:21
  9.1 2.1 %collective-permute-start.11 = (f32[1,10,1]{2,1,0:T(8,128)S(1)}, f32[1,10,1]{2,1,0:T(8,128)S(1)}, u32[]{:S(2)}, u32[]{:S(2)}) collective-permute-start(f32[1,10,1]{2,1,0:T(8,128)S(1)} %get-tuple-element.74), channel_id=1, source_target_pairs={{2,0},{4,2},{6,4},{0,6},{3,1},{5,3},{7,5},{1,7},{10,8},{12,10},{14... | collective-permute-start | bytes 128 | tf_op jit(solution)/shard_map/ppermute | solution.py:24
  11.2 1.7 %collective-permute-done.10 = f32[1,10,1]{2,1,0:T(8,128)S(1)} collective-permute-done((f32[1,10,1]{2,1,0:T(8,128)S(1)}, f32[1,10,1]{2,1,0:T(8,128)S(1)}, u32[]{:S(2)}, u32[]{:S(2)}) %collective-permute-start.10) | collective-permute-done | bytes 72 | tf_op jit(solution)/shard_map/ppermute | solution.py:21
  13.5 1.5 %collective-permute-start.2 = (f32[2,1,8,4,1]{4,2,3,1,0:T(8,128)S(1)}, f32[2,1,8,4,1]{4,2,3,1,0:T(8,128)S(1)}, u32[]{:S(2)}, u32[]{:S(2)}) collective-permute-start(f32[2,1,8,4,1]{4,2,3,1,0:T(8,128)S(1)} %get-tuple-element.55), channel_id=1, source_target_pairs={{0,2},{2,4},{4,6},{6,0},{1,3},{3,5},{5,7},{7,1},{8,10},{10,12},{12... | collective-permute-start | bytes 776 | tf_op jit(solution)/shard_map/ppermute | solution.py:21
  15.0 2.4 %collective-permute-start.3 = (f32[2,1,8,4,1]{4,2,3,1,0:T(8,128)S(1)}, f32[2,1,8,4,1]{4,2,3,1,0:T(8,128)S(1)}, u32[]{:S(2)}, u32[]{:S(2)}) collective-permute-start(f32[2,1,8,4,1]{4,2,3,1,0:T(8,128)S(1)} %get-tuple-element.56), channel_id=1, source_target_pairs={{2,0},{4,2},{6,4},{0,6},{3,1},{5,3},{7,5},{1,7},{10,8},{12,10},{14... | collective-permute-start | bytes 776 | tf_op jit(solution)/shard_map/ppermute | solution.py:24
  17.7 1.6 %collective-permute-done.2 = f32[2,1,8,4,1]{4,2,3,1,0:T(8,128)S(1)} collective-permute-done((f32[2,1,8,4,1]{4,2,3,1,0:T(8,128)S(1)}, f32[2,1,8,4,1]{4,2,3,1,0:T(8,128)S(1)}, u32[]{:S(2)}, u32[]{:S(2)}) %collective-permute-start.2) | collective-permute-done | bytes 288 | tf_op jit(solution)/shard_map/ppermute | solution.py:21
  20.7 1.7 %collective-permute-start.5 = (f32[1,8,1,128]{3,2,1,0:T(1,128)S(1)}, f32[1,8,1,128]{3,2,1,0:T(1,128)S(1)}, u32[]{:S(2)}, u32[]{:S(2)}) collective-permute-start(f32[1,8,1,128]{3,2,1,0:T(1,128)S(1)} %get-tuple-element.54), channel_id=1, source_target_pairs={{8,0},{16,8},{24,16},{0,24},{9,1},{17,9},{25,17},{1,25},{10,2},{18... | collective-permute-start | bytes 12296 | tf_op jit(solution)/shard_map/ppermute | solution.py:24
  22.7 0.3 copy.232
  23.0 0.8 collective-permute-done.4
  23.9 1.2 %collective-permute-start.6 = (f32[1,8,10,1]{3,2,1,0:T(8,128)S(1)}, f32[1,8,10,1]{3,2,1,0:T(8,128)S(1)}, u32[]{:S(2)}, u32[]{:S(2)}) collective-permute-start(f32[1,8,10,1]{3,2,1,0:T(8,128)S(1)} %get-tuple-element.43), channel_id=1, source_target_pairs={{0,2},{2,4},{4,6},{6,0},{1,3},{3,5},{5,7},{7,1},{8,10},{10,12},{12... | collective-permute-start | bytes 968 | tf_op jit(solution)/shard_map/ppermute | solution.py:21
  25.1 2.6 %collective-permute-start.7 = (f32[1,8,10,1]{3,2,1,0:T(8,128)S(1)}, f32[1,8,10,1]{3,2,1,0:T(8,128)S(1)}, u32[]{:S(2)}, u32[]{:S(2)}) collective-permute-start(f32[1,8,10,1]{3,2,1,0:T(8,128)S(1)} %get-tuple-element.44), channel_id=1, source_target_pairs={{2,0},{4,2},{6,4},{0,6},{3,1},{5,3},{7,5},{1,7},{10,8},{12,10},{14... | collective-permute-start | bytes 968 | tf_op jit(solution)/shard_map/ppermute | solution.py:24
  27.9 2.1 %collective-permute-done.6 = f32[1,8,10,1]{3,2,1,0:T(8,128)S(1)} collective-permute-done((f32[1,8,10,1]{3,2,1,0:T(8,128)S(1)}, f32[1,8,10,1]{3,2,1,0:T(8,128)S(1)}, u32[]{:S(2)}, u32[]{:S(2)}) %collective-permute-start.6) | collective-permute-done | bytes 352 | tf_op jit(solution)/shard_map/ppermute | solution.py:21
  30.6 0.4 copy.229
  31.0 0.4 fusion.50
  31.4 0.3 slice.423
  31.7 0.7 slice_add_fusion.7
  32.4 0.9 %pad_maximum_fusion = f32[1,8,16,34,4]{1,4,3,2,0:T(4,128)S(1)} fusion(f32[1,8,16,34,1]{1,4,3,2,0:T(1,128)S(1)} %get-tuple-element.20, f32[1,8,16,34,2]{1,4,3,2,0:T(2,128)S(1)} %slice.423, f32[1,8,16,34,1]{1,4,3,2,0:T(1,128)S(1)} %get-tuple-element.19), kind=kLoop, calls=%fused_computation | loop fusion | flops 34816 | bytes 139264 | tf_op jit(solution)/shard_map/concatenate | solution.py:70
  33.8 0.3 fusion.46
  34.3 1.1 %collective-permute-start.12 = (f32[2,1,8,1,32]{4,2,3,1,0:T(8,128)S(1)}, f32[2,1,8,1,32]{4,2,3,1,0:T(8,128)S(1)}, u32[]{:S(2)}, u32[]{:S(2)}) collective-permute-start(f32[2,1,8,1,32]{4,2,3,1,0:T(8,128)S(1)} %get-tuple-element.63), channel_id=1, source_target_pairs={{0,8},{8,16},{16,24},{24,0},{1,9},{9,17},{17,25},{25,1},{2,10},{10... | collective-permute-start | bytes 6152 | tf_op jit(solution)/shard_map/ppermute | solution.py:21
  35.3 0.7 collective-permute-start.13
  36.0 1.3 %collective-permute-done.12 = f32[2,1,8,1,32]{4,2,3,1,0:T(8,128)S(1)} collective-permute-done((f32[2,1,8,1,32]{4,2,3,1,0:T(8,128)S(1)}, f32[2,1,8,1,32]{4,2,3,1,0:T(8,128)S(1)}, u32[]{:S(2)}, u32[]{:S(2)}) %collective-permute-start.12) | collective-permute-done | bytes 2080 | tf_op jit(solution)/shard_map/ppermute | solution.py:21
  37.5 2.0 %collective-permute-start.14 = (f32[2,1,8,4,1]{4,2,3,1,0:T(8,128)S(1)}, f32[2,1,8,4,1]{4,2,3,1,0:T(8,128)S(1)}, u32[]{:S(2)}, u32[]{:S(2)}) collective-permute-start(f32[2,1,8,4,1]{4,2,3,1,0:T(8,128)S(1)} %get-tuple-element.51), channel_id=1, source_target_pairs={{0,2},{2,4},{4,6},{6,0},{1,3},{3,5},{5,7},{7,1},{8,10},{10,12},{12... | collective-permute-start | bytes 776 | tf_op jit(solution)/shard_map/ppermute | solution.py:21
  39.5 1.8 %collective-permute-start.15 = (f32[2,1,8,4,1]{4,2,3,1,0:T(8,128)S(1)}, f32[2,1,8,4,1]{4,2,3,1,0:T(8,128)S(1)}, u32[]{:S(2)}, u32[]{:S(2)}) collective-permute-start(f32[2,1,8,4,1]{4,2,3,1,0:T(8,128)S(1)} %get-tuple-element.52), channel_id=1, source_target_pairs={{2,0},{4,2},{6,4},{0,6},{3,1},{5,3},{7,5},{1,7},{10,8},{12,10},{14... | collective-permute-start | bytes 776 | tf_op jit(solution)/shard_map/ppermute | solution.py:24
  41.4 1.7 %collective-permute-done.14 = f32[2,1,8,4,1]{4,2,3,1,0:T(8,128)S(1)} collective-permute-done((f32[2,1,8,4,1]{4,2,3,1,0:T(8,128)S(1)}, f32[2,1,8,4,1]{4,2,3,1,0:T(8,128)S(1)}, u32[]{:S(2)}, u32[]{:S(2)}) %collective-permute-start.14) | collective-permute-done | bytes 288 | tf_op jit(solution)/shard_map/ppermute | solution.py:21
  43.2 0.3 collective-permute-done.15
  44.4 0.3 fusion.11
  44.7 1.0 %collective-permute-start.16 = (f32[1,8,1,128]{3,2,1,0:T(1,128)S(1)}, f32[1,8,1,128]{3,2,1,0:T(1,128)S(1)}, u32[]{:S(2)}, u32[]{:S(2)}) collective-permute-start(f32[1,8,1,128]{3,2,1,0:T(1,128)S(1)} %get-tuple-element.49), channel_id=1, source_target_pairs={{0,8},{8,16},{16,24},{24,0},{1,9},{9,17},{17,25},{25,1},{2,10},{10... | collective-permute-start | bytes 12296 | tf_op jit(solution)/shard_map/ppermute | solution.py:21
  45.6 0.8 collective-permute-start.17
  46.5 1.3 %collective-permute-done.16 = f32[1,8,1,128]{3,2,1,0:T(1,128)S(1)} collective-permute-done((f32[1,8,1,128]{3,2,1,0:T(1,128)S(1)}, f32[1,8,1,128]{3,2,1,0:T(1,128)S(1)}, u32[]{:S(2)}, u32[]{:S(2)}) %collective-permute-start.16) | collective-permute-done | bytes 4128 | tf_op jit(solution)/shard_map/ppermute | solution.py:21
  47.9 1.0 %collective-permute-start.18 = (f32[1,8,10,1]{3,2,1,0:T(8,128)S(1)}, f32[1,8,10,1]{3,2,1,0:T(8,128)S(1)}, u32[]{:S(2)}, u32[]{:S(2)}) collective-permute-start(f32[1,8,10,1]{3,2,1,0:T(8,128)S(1)} %get-tuple-element.41), channel_id=1, source_target_pairs={{0,2},{2,4},{4,6},{6,0},{1,3},{3,5},{5,7},{7,1},{8,10},{10,12},{12... | collective-permute-start | bytes 968 | tf_op jit(solution)/shard_map/ppermute | solution.py:21
  48.9 2.8 %collective-permute-start.19 = (f32[1,8,10,1]{3,2,1,0:T(8,128)S(1)}, f32[1,8,10,1]{3,2,1,0:T(8,128)S(1)}, u32[]{:S(2)}, u32[]{:S(2)}) collective-permute-start(f32[1,8,10,1]{3,2,1,0:T(8,128)S(1)} %get-tuple-element.42), channel_id=1, source_target_pairs={{2,0},{4,2},{6,4},{0,6},{3,1},{5,3},{7,5},{1,7},{10,8},{12,10},{14... | collective-permute-start | bytes 968 | tf_op jit(solution)/shard_map/ppermute | solution.py:24
  51.7 2.3 %collective-permute-done.18 = f32[1,8,10,1]{3,2,1,0:T(8,128)S(1)} collective-permute-done((f32[1,8,10,1]{3,2,1,0:T(8,128)S(1)}, f32[1,8,10,1]{3,2,1,0:T(8,128)S(1)}, u32[]{:S(2)}, u32[]{:S(2)}) %collective-permute-start.18) | collective-permute-done | bytes 352 | tf_op jit(solution)/shard_map/ppermute | solution.py:21
  54.5 0.4 copy.246
  54.8 0.4 fusion.49
  55.2 0.3 slice.463
  55.5 0.7 slice_add_fusion.5
  56.2 0.9 %pad_maximum_fusion.1 = f32[1,8,16,34,4]{1,4,3,2,0:T(4,128)S(1)} fusion(f32[1,8,16,34,1]{1,4,3,2,0:T(1,128)S(1)} %get-tuple-element.16, f32[1,8,16,34,2]{1,4,3,2,0:T(2,128)S(1)} %slice.463, f32[1,8,16,34,1]{1,4,3,2,0:T(1,128)S(1)} %get-tuple-element.15), kind=kLoop, calls=%fused_computation.1 | loop fusion | flops 34816 | bytes 139264 | tf_op jit(solution)/shard_map/concatenate | solution.py:70
  57.6 0.3 fusion.45
  58.1 1.4 %collective-permute-start.20 = (f32[2,1,8,1,32]{4,2,3,1,0:T(8,128)S(1)}, f32[2,1,8,1,32]{4,2,3,1,0:T(8,128)S(1)}, u32[]{:S(2)}, u32[]{:S(2)}) collective-permute-start(f32[2,1,8,1,32]{4,2,3,1,0:T(8,128)S(1)} %get-tuple-element.59), channel_id=1, source_target_pairs={{0,8},{8,16},{16,24},{24,0},{1,9},{9,17},{17,25},{25,1},{2,10},{10... | collective-permute-start | bytes 6152 | tf_op jit(solution)/shard_map/ppermute | solution.py:21
  59.5 0.4 collective-permute-start.21
  59.9 1.3 %collective-permute-done.20 = f32[2,1,8,1,32]{4,2,3,1,0:T(8,128)S(1)} collective-permute-done((f32[2,1,8,1,32]{4,2,3,1,0:T(8,128)S(1)}, f32[2,1,8,1,32]{4,2,3,1,0:T(8,128)S(1)}, u32[]{:S(2)}, u32[]{:S(2)}) %collective-permute-start.20) | collective-permute-done | bytes 2080 | tf_op jit(solution)/shard_map/ppermute | solution.py:21
  61.3 1.8 %collective-permute-start.22 = (f32[2,1,8,4,1]{4,2,3,1,0:T(8,128)S(1)}, f32[2,1,8,4,1]{4,2,3,1,0:T(8,128)S(1)}, u32[]{:S(2)}, u32[]{:S(2)}) collective-permute-start(f32[2,1,8,4,1]{4,2,3,1,0:T(8,128)S(1)} %get-tuple-element.47), channel_id=1, source_target_pairs={{0,2},{2,4},{4,6},{6,0},{1,3},{3,5},{5,7},{7,1},{8,10},{10,12},{12... | collective-permute-start | bytes 776 | tf_op jit(solution)/shard_map/ppermute | solution.py:21
  63.1 2.0 %collective-permute-start.23 = (f32[2,1,8,4,1]{4,2,3,1,0:T(8,128)S(1)}, f32[2,1,8,4,1]{4,2,3,1,0:T(8,128)S(1)}, u32[]{:S(2)}, u32[]{:S(2)}) collective-permute-start(f32[2,1,8,4,1]{4,2,3,1,0:T(8,128)S(1)} %get-tuple-element.48), channel_id=1, source_target_pairs={{2,0},{4,2},{6,4},{0,6},{3,1},{5,3},{7,5},{1,7},{10,8},{12,10},{14... | collective-permute-start | bytes 776 | tf_op jit(solution)/shard_map/ppermute | solution.py:24
  65.3 1.8 %collective-permute-done.22 = f32[2,1,8,4,1]{4,2,3,1,0:T(8,128)S(1)} collective-permute-done((f32[2,1,8,4,1]{4,2,3,1,0:T(8,128)S(1)}, f32[2,1,8,4,1]{4,2,3,1,0:T(8,128)S(1)}, u32[]{:S(2)}, u32[]{:S(2)}) %collective-permute-start.22) | collective-permute-done | bytes 288 | tf_op jit(solution)/shard_map/ppermute | solution.py:21
  68.5 1.0 %collective-permute-start.24 = (f32[1,8,1,128]{3,2,1,0:T(1,128)S(1)}, f32[1,8,1,128]{3,2,1,0:T(1,128)S(1)}, u32[]{:S(2)}, u32[]{:S(2)}) collective-permute-start(f32[1,8,1,128]{3,2,1,0:T(1,128)S(1)} %get-tuple-element.45), channel_id=1, source_target_pairs={{0,8},{8,16},{16,24},{24,0},{1,9},{9,17},{17,25},{25,1},{2,10},{10... | collective-permute-start | bytes 12296 | tf_op jit(solution)/shard_map/ppermute | solution.py:21
  69.5 0.8 collective-permute-start.25
  70.3 1.3 %collective-permute-done.24 = f32[1,8,1,128]{3,2,1,0:T(1,128)S(1)} collective-permute-done((f32[1,8,1,128]{3,2,1,0:T(1,128)S(1)}, f32[1,8,1,128]{3,2,1,0:T(1,128)S(1)}, u32[]{:S(2)}, u32[]{:S(2)}) %collective-permute-start.24) | collective-permute-done | bytes 4128 | tf_op jit(solution)/shard_map/ppermute | solution.py:21
  71.7 0.9 %collective-permute-start.26 = (f32[1,8,10,1]{3,2,1,0:T(8,128)S(1)}, f32[1,8,10,1]{3,2,1,0:T(8,128)S(1)}, u32[]{:S(2)}, u32[]{:S(2)}) collective-permute-start(f32[1,8,10,1]{3,2,1,0:T(8,128)S(1)} %get-tuple-element.39), channel_id=1, source_target_pairs={{0,2},{2,4},{4,6},{6,0},{1,3},{3,5},{5,7},{7,1},{8,10},{10,12},{12... | collective-permute-start | bytes 968 | tf_op jit(solution)/shard_map/ppermute | solution.py:21
  72.6 3.0 %collective-permute-start.27 = (f32[1,8,10,1]{3,2,1,0:T(8,128)S(1)}, f32[1,8,10,1]{3,2,1,0:T(8,128)S(1)}, u32[]{:S(2)}, u32[]{:S(2)}) collective-permute-start(f32[1,8,10,1]{3,2,1,0:T(8,128)S(1)} %get-tuple-element.40), channel_id=1, source_target_pairs={{2,0},{4,2},{6,4},{0,6},{3,1},{5,3},{7,5},{1,7},{10,8},{12,10},{14... | collective-permute-start | bytes 968 | tf_op jit(solution)/shard_map/ppermute | solution.py:24
  75.6 2.3 %collective-permute-done.26 = f32[1,8,10,1]{3,2,1,0:T(8,128)S(1)} collective-permute-done((f32[1,8,10,1]{3,2,1,0:T(8,128)S(1)}, f32[1,8,10,1]{3,2,1,0:T(8,128)S(1)}, u32[]{:S(2)}, u32[]{:S(2)}) %collective-permute-start.26) | collective-permute-done | bytes 352 | tf_op jit(solution)/shard_map/ppermute | solution.py:21
  78.2 0.4 copy.261
  78.6 0.4 fusion.48
  79.0 0.3 slice.490
  79.3 0.7 slice_add_fusion.3
  80.0 0.9 %pad_maximum_fusion.2 = f32[1,8,16,34,4]{1,4,3,2,0:T(4,128)S(1)} fusion(f32[1,8,16,34,1]{1,4,3,2,0:T(1,128)S(1)} %get-tuple-element.12, f32[1,8,16,34,2]{1,4,3,2,0:T(2,128)S(1)} %slice.490, f32[1,8,16,34,1]{1,4,3,2,0:T(1,128)S(1)} %get-tuple-element.11), kind=kLoop, calls=%fused_computation.2 | loop fusion | flops 34816 | bytes 139264 | tf_op jit(solution)/shard_map/concatenate | solution.py:70
  81.2 6.7 %all_to_all.12 = f32[1,8,8,128]{3,2,0,1:T(8,128)S(1)} all-to-all(f32[1,8,8,128]{3,2,0,1:T(8,128)S(1)} %add_bitcast_fusion), channel_id=1, replica_groups=mesh['px'=4,'py'=4,'lev'=2] {'lev'}, dimensions={1} | all-to-all | bytes 65536 | tf_op jit(solution)/shard_map/all_to_all | solution.py:148
  88.1 0.6 copy.266
  (144 shorter events, 9.0 us)
Async XLA Ops:
  0.0 87.8 %copy-start = (f32[2,2]{1,0:T(2,128)S(1)}, f32[2,2]{1,0:T(2,128)}, u32[]{:S(2)}) copy-start(f32[2,2]{1,0:T(2,128)} %param.11) | copy-start | bytes 52
  0.0 6.4 %copy-start.5 = (f32[8,8,1]{1,0,2:T(8,128)S(1)}, f32[8,8,1]{1,0,2:T(8,128)}, u32[]{:S(2)}) copy-start(f32[8,8,1]{1,0,2:T(8,128)} %constant.100) | copy-start | bytes 772
  0.0 6.6 %copy-start.3 = (f32[1,8,128]{2,1,0:T(8,128)S(1)}, f32[1,8,128]{2,1,0:T(8,128)}, u32[]{:S(2)}) copy-start(f32[1,8,128]{2,1,0:T(8,128)} %param.8) | copy-start | bytes 12292
  0.0 6.4 %copy-start.1 = (f32[1,8,8,128]{3,2,1,0:T(8,128)S(1)}, f32[1,8,8,128]{3,2,1,0:T(8,128)}, u32[]{:S(2)}) copy-start(f32[1,8,8,128]{3,2,1,0:T(8,128)} %param.7) | copy-start | bytes 98308
  0.0 6.4 %copy-start.4 = (f32[1,8,128]{2,1,0:T(8,128)S(1)}, f32[1,8,128]{2,1,0:T(8,128)}, u32[]{:S(2)}) copy-start(f32[1,8,128]{2,1,0:T(8,128)} %param.9) | copy-start | bytes 12292
  0.8 5.8 %collective-permute-start.8 = (f32[1,1,128]{2,1,0:T(1,128)S(1)}, f32[1,1,128]{2,1,0:T(1,128)S(1)}, u32[]{:S(2)}, u32[]{:S(2)}) collective-permute-start(f32[1,1,128]{2,1,0:T(1,128)S(1)} %get-tuple-element.75), channel_id=1, source_target_pairs={{0,8},{8,16},{16,24},{24,0},{1,9},{9,17},{17,25},{25,1},{2,10},{10... | collective-permute-start | bytes 1544 | tf_op jit(solution)/shard_map/ppermute | solution.py:21
  1.3 5.4 %collective-permute-start.9 = (f32[1,1,128]{2,1,0:T(1,128)S(1)}, f32[1,1,128]{2,1,0:T(1,128)S(1)}, u32[]{:S(2)}, u32[]{:S(2)}) collective-permute-start(f32[1,1,128]{2,1,0:T(1,128)S(1)} %get-tuple-element.76), channel_id=1, source_target_pairs={{8,0},{16,8},{24,16},{0,24},{9,1},{17,9},{25,17},{1,25},{10,2},{18... | collective-permute-start | bytes 1544 | tf_op jit(solution)/shard_map/ppermute | solution.py:24
  4.7 8.7 %collective-permute-start = (f32[2,1,8,1,32]{4,2,3,1,0:T(8,128)S(1)}, f32[2,1,8,1,32]{4,2,3,1,0:T(8,128)S(1)}, u32[]{:S(2)}, u32[]{:S(2)}) collective-permute-start(f32[2,1,8,1,32]{4,2,3,1,0:T(8,128)S(1)} %get-tuple-element.71), channel_id=1, source_target_pairs={{0,8},{8,16},{16,24},{24,0},{1,9},{9,17},{17,25},{25,1},{2,10},{10... | collective-permute-start | bytes 6152 | tf_op jit(solution)/shard_map/ppermute | solution.py:21
  5.3 8.1 %collective-permute-start.1 = (f32[2,1,8,1,32]{4,2,3,1,0:T(8,128)S(1)}, f32[2,1,8,1,32]{4,2,3,1,0:T(8,128)S(1)}, u32[]{:S(2)}, u32[]{:S(2)}) collective-permute-start(f32[2,1,8,1,32]{4,2,3,1,0:T(8,128)S(1)} %get-tuple-element.72), channel_id=1, source_target_pairs={{8,0},{16,8},{24,16},{0,24},{9,1},{17,9},{25,17},{1,25},{10,2},{18... | collective-permute-start | bytes 6152 | tf_op jit(solution)/shard_map/ppermute | solution.py:24
  6.8 6.1 %collective-permute-start.10 = (f32[1,10,1]{2,1,0:T(8,128)S(1)}, f32[1,10,1]{2,1,0:T(8,128)S(1)}, u32[]{:S(2)}, u32[]{:S(2)}) collective-permute-start(f32[1,10,1]{2,1,0:T(8,128)S(1)} %get-tuple-element.73), channel_id=1, source_target_pairs={{0,2},{2,4},{4,6},{6,0},{1,3},{3,5},{5,7},{7,1},{8,10},{10,12},{12... | collective-permute-start | bytes 128 | tf_op jit(solution)/shard_map/ppermute | solution.py:21
  9.1 3.7 %collective-permute-start.11 = (f32[1,10,1]{2,1,0:T(8,128)S(1)}, f32[1,10,1]{2,1,0:T(8,128)S(1)}, u32[]{:S(2)}, u32[]{:S(2)}) collective-permute-start(f32[1,10,1]{2,1,0:T(8,128)S(1)} %get-tuple-element.74), channel_id=1, source_target_pairs={{2,0},{4,2},{6,4},{0,6},{3,1},{5,3},{7,5},{1,7},{10,8},{12,10},{14... | collective-permute-start | bytes 128 | tf_op jit(solution)/shard_map/ppermute | solution.py:24
  13.5 5.8 %collective-permute-start.2 = (f32[2,1,8,4,1]{4,2,3,1,0:T(8,128)S(1)}, f32[2,1,8,4,1]{4,2,3,1,0:T(8,128)S(1)}, u32[]{:S(2)}, u32[]{:S(2)}) collective-permute-start(f32[2,1,8,4,1]{4,2,3,1,0:T(8,128)S(1)} %get-tuple-element.55), channel_id=1, source_target_pairs={{0,2},{2,4},{4,6},{6,0},{1,3},{3,5},{5,7},{7,1},{8,10},{10,12},{12... | collective-permute-start | bytes 776 | tf_op jit(solution)/shard_map/ppermute | solution.py:21
  15.0 4.3 %collective-permute-start.3 = (f32[2,1,8,4,1]{4,2,3,1,0:T(8,128)S(1)}, f32[2,1,8,4,1]{4,2,3,1,0:T(8,128)S(1)}, u32[]{:S(2)}, u32[]{:S(2)}) collective-permute-start(f32[2,1,8,4,1]{4,2,3,1,0:T(8,128)S(1)} %get-tuple-element.56), channel_id=1, source_target_pairs={{2,0},{4,2},{6,4},{0,6},{3,1},{5,3},{7,5},{1,7},{10,8},{12,10},{14... | collective-permute-start | bytes 776 | tf_op jit(solution)/shard_map/ppermute | solution.py:24
  19.5 0.9 copy-start.2
  19.5 0.8 copy-start.6
  20.7 3.1 %collective-permute-start.4 = (f32[1,8,1,128]{3,2,1,0:T(1,128)S(1)}, f32[1,8,1,128]{3,2,1,0:T(1,128)S(1)}, u32[]{:S(2)}, u32[]{:S(2)}) collective-permute-start(f32[1,8,1,128]{3,2,1,0:T(1,128)S(1)} %get-tuple-element.53), channel_id=1, source_target_pairs={{0,8},{8,16},{16,24},{24,0},{1,9},{9,17},{17,25},{25,1},{2,10},{10... | collective-permute-start | bytes 12296 | tf_op jit(solution)/shard_map/ppermute | solution.py:21
  20.7 3.1 %collective-permute-start.5 = (f32[1,8,1,128]{3,2,1,0:T(1,128)S(1)}, f32[1,8,1,128]{3,2,1,0:T(1,128)S(1)}, u32[]{:S(2)}, u32[]{:S(2)}) collective-permute-start(f32[1,8,1,128]{3,2,1,0:T(1,128)S(1)} %get-tuple-element.54), channel_id=1, source_target_pairs={{8,0},{16,8},{24,16},{0,24},{9,1},{17,9},{25,17},{1,25},{10,2},{18... | collective-permute-start | bytes 12296 | tf_op jit(solution)/shard_map/ppermute | solution.py:24
  23.9 6.2 %collective-permute-start.6 = (f32[1,8,10,1]{3,2,1,0:T(8,128)S(1)}, f32[1,8,10,1]{3,2,1,0:T(8,128)S(1)}, u32[]{:S(2)}, u32[]{:S(2)}) collective-permute-start(f32[1,8,10,1]{3,2,1,0:T(8,128)S(1)} %get-tuple-element.43), channel_id=1, source_target_pairs={{0,2},{2,4},{4,6},{6,0},{1,3},{3,5},{5,7},{7,1},{8,10},{10,12},{12... | collective-permute-start | bytes 968 | tf_op jit(solution)/shard_map/ppermute | solution.py:21
  25.1 5.1 %collective-permute-start.7 = (f32[1,8,10,1]{3,2,1,0:T(8,128)S(1)}, f32[1,8,10,1]{3,2,1,0:T(8,128)S(1)}, u32[]{:S(2)}, u32[]{:S(2)}) collective-permute-start(f32[1,8,10,1]{3,2,1,0:T(8,128)S(1)} %get-tuple-element.44), channel_id=1, source_target_pairs={{2,0},{4,2},{6,4},{0,6},{3,1},{5,3},{7,5},{1,7},{10,8},{12,10},{14... | collective-permute-start | bytes 968 | tf_op jit(solution)/shard_map/ppermute | solution.py:24
  34.3 3.1 %collective-permute-start.12 = (f32[2,1,8,1,32]{4,2,3,1,0:T(8,128)S(1)}, f32[2,1,8,1,32]{4,2,3,1,0:T(8,128)S(1)}, u32[]{:S(2)}, u32[]{:S(2)}) collective-permute-start(f32[2,1,8,1,32]{4,2,3,1,0:T(8,128)S(1)} %get-tuple-element.63), channel_id=1, source_target_pairs={{0,8},{8,16},{16,24},{24,0},{1,9},{9,17},{17,25},{25,1},{2,10},{10... | collective-permute-start | bytes 6152 | tf_op jit(solution)/shard_map/ppermute | solution.py:21
  35.3 2.0 %collective-permute-start.13 = (f32[2,1,8,1,32]{4,2,3,1,0:T(8,128)S(1)}, f32[2,1,8,1,32]{4,2,3,1,0:T(8,128)S(1)}, u32[]{:S(2)}, u32[]{:S(2)}) collective-permute-start(f32[2,1,8,1,32]{4,2,3,1,0:T(8,128)S(1)} %get-tuple-element.64), channel_id=1, source_target_pairs={{8,0},{16,8},{24,16},{0,24},{9,1},{17,9},{25,17},{1,25},{10,2},{18... | collective-permute-start | bytes 6152 | tf_op jit(solution)/shard_map/ppermute | solution.py:24
  37.5 5.7 %collective-permute-start.14 = (f32[2,1,8,4,1]{4,2,3,1,0:T(8,128)S(1)}, f32[2,1,8,4,1]{4,2,3,1,0:T(8,128)S(1)}, u32[]{:S(2)}, u32[]{:S(2)}) collective-permute-start(f32[2,1,8,4,1]{4,2,3,1,0:T(8,128)S(1)} %get-tuple-element.51), channel_id=1, source_target_pairs={{0,2},{2,4},{4,6},{6,0},{1,3},{3,5},{5,7},{7,1},{8,10},{10,12},{12... | collective-permute-start | bytes 776 | tf_op jit(solution)/shard_map/ppermute | solution.py:21
  39.5 4.0 %collective-permute-start.15 = (f32[2,1,8,4,1]{4,2,3,1,0:T(8,128)S(1)}, f32[2,1,8,4,1]{4,2,3,1,0:T(8,128)S(1)}, u32[]{:S(2)}, u32[]{:S(2)}) collective-permute-start(f32[2,1,8,4,1]{4,2,3,1,0:T(8,128)S(1)} %get-tuple-element.52), channel_id=1, source_target_pairs={{2,0},{4,2},{6,4},{0,6},{3,1},{5,3},{7,5},{1,7},{10,8},{12,10},{14... | collective-permute-start | bytes 776 | tf_op jit(solution)/shard_map/ppermute | solution.py:24
  44.7 3.1 %collective-permute-start.16 = (f32[1,8,1,128]{3,2,1,0:T(1,128)S(1)}, f32[1,8,1,128]{3,2,1,0:T(1,128)S(1)}, u32[]{:S(2)}, u32[]{:S(2)}) collective-permute-start(f32[1,8,1,128]{3,2,1,0:T(1,128)S(1)} %get-tuple-element.49), channel_id=1, source_target_pairs={{0,8},{8,16},{16,24},{24,0},{1,9},{9,17},{17,25},{25,1},{2,10},{10... | collective-permute-start | bytes 12296 | tf_op jit(solution)/shard_map/ppermute | solution.py:21
  45.6 2.1 %collective-permute-start.17 = (f32[1,8,1,128]{3,2,1,0:T(1,128)S(1)}, f32[1,8,1,128]{3,2,1,0:T(1,128)S(1)}, u32[]{:S(2)}, u32[]{:S(2)}) collective-permute-start(f32[1,8,1,128]{3,2,1,0:T(1,128)S(1)} %get-tuple-element.50), channel_id=1, source_target_pairs={{8,0},{16,8},{24,16},{0,24},{9,1},{17,9},{25,17},{1,25},{10,2},{18... | collective-permute-start | bytes 12296 | tf_op jit(solution)/shard_map/ppermute | solution.py:24
  47.9 6.2 %collective-permute-start.18 = (f32[1,8,10,1]{3,2,1,0:T(8,128)S(1)}, f32[1,8,10,1]{3,2,1,0:T(8,128)S(1)}, u32[]{:S(2)}, u32[]{:S(2)}) collective-permute-start(f32[1,8,10,1]{3,2,1,0:T(8,128)S(1)} %get-tuple-element.41), channel_id=1, source_target_pairs={{0,2},{2,4},{4,6},{6,0},{1,3},{3,5},{5,7},{7,1},{8,10},{10,12},{12... | collective-permute-start | bytes 968 | tf_op jit(solution)/shard_map/ppermute | solution.py:21
  48.9 5.2 %collective-permute-start.19 = (f32[1,8,10,1]{3,2,1,0:T(8,128)S(1)}, f32[1,8,10,1]{3,2,1,0:T(8,128)S(1)}, u32[]{:S(2)}, u32[]{:S(2)}) collective-permute-start(f32[1,8,10,1]{3,2,1,0:T(8,128)S(1)} %get-tuple-element.42), channel_id=1, source_target_pairs={{2,0},{4,2},{6,4},{0,6},{3,1},{5,3},{7,5},{1,7},{10,8},{12,10},{14... | collective-permute-start | bytes 968 | tf_op jit(solution)/shard_map/ppermute | solution.py:24
  58.1 3.1 %collective-permute-start.20 = (f32[2,1,8,1,32]{4,2,3,1,0:T(8,128)S(1)}, f32[2,1,8,1,32]{4,2,3,1,0:T(8,128)S(1)}, u32[]{:S(2)}, u32[]{:S(2)}) collective-permute-start(f32[2,1,8,1,32]{4,2,3,1,0:T(8,128)S(1)} %get-tuple-element.59), channel_id=1, source_target_pairs={{0,8},{8,16},{16,24},{24,0},{1,9},{9,17},{17,25},{25,1},{2,10},{10... | collective-permute-start | bytes 6152 | tf_op jit(solution)/shard_map/ppermute | solution.py:21
  59.5 1.7 %collective-permute-start.21 = (f32[2,1,8,1,32]{4,2,3,1,0:T(8,128)S(1)}, f32[2,1,8,1,32]{4,2,3,1,0:T(8,128)S(1)}, u32[]{:S(2)}, u32[]{:S(2)}) collective-permute-start(f32[2,1,8,1,32]{4,2,3,1,0:T(8,128)S(1)} %get-tuple-element.60), channel_id=1, source_target_pairs={{8,0},{16,8},{24,16},{0,24},{9,1},{17,9},{25,17},{1,25},{10,2},{18... | collective-permute-start | bytes 6152 | tf_op jit(solution)/shard_map/ppermute | solution.py:24
  61.3 5.8 %collective-permute-start.22 = (f32[2,1,8,4,1]{4,2,3,1,0:T(8,128)S(1)}, f32[2,1,8,4,1]{4,2,3,1,0:T(8,128)S(1)}, u32[]{:S(2)}, u32[]{:S(2)}) collective-permute-start(f32[2,1,8,4,1]{4,2,3,1,0:T(8,128)S(1)} %get-tuple-element.47), channel_id=1, source_target_pairs={{0,2},{2,4},{4,6},{6,0},{1,3},{3,5},{5,7},{7,1},{8,10},{10,12},{12... | collective-permute-start | bytes 776 | tf_op jit(solution)/shard_map/ppermute | solution.py:21
  63.1 4.3 %collective-permute-start.23 = (f32[2,1,8,4,1]{4,2,3,1,0:T(8,128)S(1)}, f32[2,1,8,4,1]{4,2,3,1,0:T(8,128)S(1)}, u32[]{:S(2)}, u32[]{:S(2)}) collective-permute-start(f32[2,1,8,4,1]{4,2,3,1,0:T(8,128)S(1)} %get-tuple-element.48), channel_id=1, source_target_pairs={{2,0},{4,2},{6,4},{0,6},{3,1},{5,3},{7,5},{1,7},{10,8},{12,10},{14... | collective-permute-start | bytes 776 | tf_op jit(solution)/shard_map/ppermute | solution.py:24
  68.5 3.1 %collective-permute-start.24 = (f32[1,8,1,128]{3,2,1,0:T(1,128)S(1)}, f32[1,8,1,128]{3,2,1,0:T(1,128)S(1)}, u32[]{:S(2)}, u32[]{:S(2)}) collective-permute-start(f32[1,8,1,128]{3,2,1,0:T(1,128)S(1)} %get-tuple-element.45), channel_id=1, source_target_pairs={{0,8},{8,16},{16,24},{24,0},{1,9},{9,17},{17,25},{25,1},{2,10},{10... | collective-permute-start | bytes 12296 | tf_op jit(solution)/shard_map/ppermute | solution.py:21
  69.5 2.2 %collective-permute-start.25 = (f32[1,8,1,128]{3,2,1,0:T(1,128)S(1)}, f32[1,8,1,128]{3,2,1,0:T(1,128)S(1)}, u32[]{:S(2)}, u32[]{:S(2)}) collective-permute-start(f32[1,8,1,128]{3,2,1,0:T(1,128)S(1)} %get-tuple-element.46), channel_id=1, source_target_pairs={{8,0},{16,8},{24,16},{0,24},{9,1},{17,9},{25,17},{1,25},{10,2},{18... | collective-permute-start | bytes 12296 | tf_op jit(solution)/shard_map/ppermute | solution.py:24
  71.7 6.1 %collective-permute-start.26 = (f32[1,8,10,1]{3,2,1,0:T(8,128)S(1)}, f32[1,8,10,1]{3,2,1,0:T(8,128)S(1)}, u32[]{:S(2)}, u32[]{:S(2)}) collective-permute-start(f32[1,8,10,1]{3,2,1,0:T(8,128)S(1)} %get-tuple-element.39), channel_id=1, source_target_pairs={{0,2},{2,4},{4,6},{6,0},{1,3},{3,5},{5,7},{7,1},{8,10},{10,12},{12... | collective-permute-start | bytes 968 | tf_op jit(solution)/shard_map/ppermute | solution.py:21
  72.6 5.3 %collective-permute-start.27 = (f32[1,8,10,1]{3,2,1,0:T(8,128)S(1)}, f32[1,8,10,1]{3,2,1,0:T(8,128)S(1)}, u32[]{:S(2)}, u32[]{:S(2)}) collective-permute-start(f32[1,8,10,1]{3,2,1,0:T(8,128)S(1)} %get-tuple-element.40), channel_id=1, source_target_pairs={{2,0},{4,2},{6,4},{0,6},{3,1},{5,3},{7,5},{1,7},{10,8},{12,10},{14... | collective-permute-start | bytes 968 | tf_op jit(solution)/shard_map/ppermute | solution.py:24
where the time goes:
time: 89 us; the launch traced here: 88.7 us
  starting transfers between devices  40.6 us (46%)
  waiting for transfers between devices  20.6 us (23%)
  local copies, waits for them, and re-layouts  11 us (12%)
  other arithmetic  7.71 us (9%)
  blocking collectives  6.65 us (7%)
  matrix products  1.48 us (2%)
    ppermute x14, starting transfers between devices, extended(): lax.ppermute(lax.slice_in_dim(block, 0, width, axis=dim), axis, backward)  24.2 us
    ppermute x14, waiting for transfers between devices, extended(): lax.ppermute(lax.slice_in_dim(block, block.shape[dim] - width, None, axis...  19.6 us
    ppermute x14, starting transfers between devices, extended(): lax.ppermute(lax.slice_in_dim(block, block.shape[dim] - width, None, axis...  16.4 us
    all_to_all x1, blocking collectives, shards(): lax.all_to_all(field, 'lev', split_axis=1, concat_axis=0, tiled=True)  6.65 us
    concatenate x8, other arithmetic, pair_sum(): jnp.concatenate([head_nodes + before, middle, tail_nodes + following], ax...  3.08 us
    add x8, other arithmetic, pair_sum(): head_nodes + before  2.37 us
    unnamed x21, local copies, waits for them, and re-layouts  1.9 us
  transfers between devices with their start and end apart: 28, of which 15 were waited for; matrix products, arithmetic and copies ran while one was open for 4% of the time, Pallas kernels for 0%

commit v1 on v0

v1 whole, which is shorter than its diff:
```python
import functools

import jax
import jax.numpy as jnp
import numpy as np
from jax import lax
from jax.experimental import pallas as pl
from jax.experimental.pallas import tpu as pltpu
from jax.sharding import PartitionSpec as P

GLL_NODES = 4
SECTION_REACH = 2
SLOTS = 64

sentinel = 1e30
step_size = 0.1
section_weights = ((0.0, 1.0), (0.75, 0.25), (1.0 / 3.0, 2.0 / 3.0))
MESH = pl.DeviceIdType.MESH


def derivative_table():
    points = np.array([-1.0, -(5.0 ** (-0.5)), 5.0 ** (-0.5), 1.0])
    number = points.shape[0]
    barycentric = np.array(
        [
            1.0
            / np.prod([points[outer] - points[inner] for inner in range(number) if inner != outer])
            for outer in range(number)
        ]
    )
    table = np.zeros((number, number))
    for outer in range(number):
        for inner in range(number):
            if inner != outer:
                table[outer, inner] = (
                    barycentric[inner] / barycentric[outer] / (points[outer] - points[inner])
                )
    for outer in range(number):
        table[outer, outer] = -np.sum(table[outer])
    return table


def rolled(values, shift, axis):
    size = values.shape[axis]
    shift %= size
    return pltpu.roll(values, shift, axis) if shift else values


def moved_by_table(values, table):
    rows = values.shape[0]
    high = values.astype(jnp.bfloat16)
    rest = values - high.astype(jnp.float32)
    middle = rest.astype(jnp.bfloat16)
    low = (rest - middle.astype(jnp.float32)).astype(jnp.bfloat16)
    terms = jnp.dot(
        jnp.concatenate([high, middle, low], axis=0), table, preferred_element_type=jnp.float32
    )
    return terms[:rows] + (terms[rows : 2 * rows] + terms[2 * rows :])


def sections(tracer, node_mass, wind_x, wind_y, inside):
    nodes = range(GLL_NODES)
    table = step_size * derivative_table()

    def node_sums(values):
        first = [values[0][j] + rolled(values[3][j], 1, 0) for j in nodes]
        last = [values[3][j] + rolled(values[0][j], -1, 0) for j in nodes]
        values = [first, values[1], values[2], last]
        return [
            [row[0] + rolled(row[3], 1, 1), row[1], row[2], row[3] + rolled(row[0], -1, 1)]
            for row in values
        ]

    def tree(combine, items):
        while len(items) > 1:
            items = [combine(*items[i : i + 2]) for i in range(0, len(items), 2)]
        return items[0]

    def around(combine, values):
        for axis in (0, 1):
            values = combine(
                combine(values, rolled(values, 1, axis)), rolled(values, -1, axis)
            )
        return values

    inverse = [
        [1.0 / jnp.where(inside, entry, 1.0) for entry in row] for row in node_sums(node_mass)
    ]
    field = tracer
    for share_start, share_new in section_weights:
        flat = [field[i][j] for i in nodes for j in nodes]
        lower = around(jnp.minimum, jnp.where(inside, tree(jnp.minimum, flat), sentinel))
        upper = around(jnp.maximum, jnp.where(inside, tree(jnp.maximum, flat), -sentinel))
        flux_x = [[wind_x[i][j] * field[i][j] for j in nodes] for i in nodes]
        flux_y = [[wind_y[i][j] * field[i][j] for j in nodes] for i in nodes]
        weighted = []
        for i in nodes:
            row = []
            for j in nodes:
                slope_x = tree(jnp.add, [float(table[i, k]) * flux_x[k][j] for k in nodes])
                slope_y = tree(jnp.add, [float(table[j, k]) * flux_y[i][k] for k in nodes])
                moved = field[i][j] - (slope_x + slope_y)
                limited = jnp.minimum(jnp.maximum(moved, lower), upper)
                row.append(node_mass[i][j] * limited)
            weighted.append(row)
        summed = node_sums(weighted)
        field = [
            [
                share_new * (summed[i][j] * inverse[i][j])
                + (share_start * tracer[i][j] if share_start else 0.0)
                for j in nodes
            ]
            for i in nodes
        ]
    return field


def kernel(
    n,
    nz,
    nlev,
    tracer_hbm,
    mass_hbm,
    wind_x_hbm,
    wind_y_hbm,
    remap,
    out,
    tracer_in,
    metric_in,
    blocks_out,
    halos_out,
    blocks,
    halos,
    spread,
    gather,
    results_out,
    results,
    in_sem,
    block_send,
    block_recv,
    halo_send,
    halo_recv,
    result_send,
    result_recv,
):
    tracers, nx, ny = tracer_in.shape
    held = tracers // n
    fields = held + 3
    half = n // nlev
    reach = SECTION_REACH * len(section_weights)
    width = reach * GLL_NODES
    elements_y = ny // GLL_NODES
    elements_x = n * nx // GLL_NODES
    lanes = spread.shape[1] // GLL_NODES
    px, py, lev = lax.axis_index("px"), lax.axis_index("py"), lax.axis_index("lev")
    has_low, has_high = py > 0, py < nz - 1
    target_lev = px // half

    def others(number):
        return [lax.rem(px + d, n) for d in range(number)]

    barrier = pltpu.get_barrier_semaphore()

    def greet(x, y, level):
        pl.semaphore_signal(barrier, inc=1, device_id=(x, y, level), device_id_type=MESH)

    for d, x in enumerate(others(n)):
        pl.when(has_low)(functools.partial(greet, x, py - 1, lev))
        pl.when(has_high)(functools.partial(greet, x, py + 1, lev))
        for step in range(nlev):
            if d or step:
                greet(x, py, lax.rem(lev + step, nlev))

    copies = [pltpu.make_async_copy(tracer_hbm.at[0], tracer_in, in_sem.at[0])]
    for k, source in enumerate((mass_hbm, wind_x_hbm, wind_y_hbm)):
        copies.append(pltpu.make_async_copy(source.at[0], metric_in.at[k], in_sem.at[k + 1]))
    for copy in copies:
        copy.start()
    for copy in copies:
        copy.wait()

    lane = lax.broadcasted_iota(jnp.int32, (nx, halos.shape[2]), 1)

    def halo_tile(group, side):
        tile = jnp.zeros(lane.shape, jnp.float32)
        for k in range(fields):
            piece = tracer_in[group * held + k] if k < held else metric_in[k - held]
            shift = width * k - (ny - width if side else 0)
            wanted = (lane >= width * k) & (lane < width * (k + 1))
            tile = jnp.where(wanted, rolled(piece, shift, 1), tile)
        return tile

    for group in range(n):
        blocks_out[group, :held] = tracer_in[group * held : (group + 1) * held]
        blocks_out[group, held:] = metric_in[...]
        for side in range(2):
            halos_out[side, group] = halo_tile(group, side)

    peers = n * nlev - 1
    pl.semaphore_wait(
        barrier, peers + n * (has_low.astype(jnp.int32) + has_high.astype(jnp.int32))
    )

    mine = pl.ds(pl.multiple_of(px * nx, nx), nx)

    def block_copy(x):
        return pltpu.make_async_remote_copy(
            src_ref=blocks_out.at[x],
            dst_ref=blocks.at[:, mine, :],
            send_sem=block_send.at[x],
            recv_sem=block_recv.at[px],
            device_id=(x, py, lev),
            device_id_type=MESH,
        )

    def halo_copy(x, side):
        return pltpu.make_async_remote_copy(
            src_ref=halos_out.at[side, x],
            dst_ref=halos.at[side, mine, :],
            send_sem=halo_send.at[side, x],
            recv_sem=halo_recv.at[side, px],
            device_id=(x, py + (1 if side else -1), lev),
            device_id_type=MESH,
        )

    sides = ((0, has_low, has_high), (1, has_high, has_low))
    for x in others(n)[1:]:
        block_copy(x).start()
    for side, sends, _ in sides:
        for x in others(n):

            @pl.when(sends)
            def _(side=side, x=x):
                halo_copy(x, side).start()

    blocks[:, mine, :] = blocks_out[px]
    for side, _, gets in sides:

        @pl.when(jnp.logical_not(gets))
        def _(side=side):
            halos[side] = jnp.zeros(halos.shape[1:], jnp.float32)

    def node_of(shape, axis):
        return lax.broadcasted_iota(jnp.int32, shape, axis)

    depth = ny + halos.shape[2]
    source = node_of((depth, 1), 0)
    slot = jnp.where(
        source < ny + width,
        reach + source // GLL_NODES,
        jnp.where(source < ny + 2 * width, (source - ny - width) // GLL_NODES, -SLOTS * lanes),
    )
    place = lax.rem(source, GLL_NODES) * lanes + slot
    column = node_of((1, spread.shape[1]), 1)
    for k in range(held):
        spread[k * depth : (k + 1) * depth] = jnp.where(
            place + k * SLOTS == column, 1.0, 0.0
        ).astype(jnp.bfloat16)
    source = node_of((gather.shape[0], 1), 0)
    at = lax.rem(source, lanes)
    element = lax.rem(at, SLOTS) - reach
    kept = (element >= 0) & (element < elements_y) & (at // SLOTS < held)
    place = jnp.where(
        kept, at // SLOTS * ny + element * GLL_NODES + source // lanes, -1
    )
    gather[...] = jnp.where(place == node_of((1, gather.shape[1]), 1), 1.0, 0.0).astype(
        jnp.bfloat16
    )

    for x in others(n)[1:]:
        rows = pl.ds(pl.multiple_of(x * nx, nx), nx)
        pltpu.make_async_remote_copy(
            src_ref=blocks_out.at[x],
            dst_ref=blocks.at[:, rows, :],
            send_sem=block_send.at[x],
            recv_sem=block_recv.at[x],
            device_id=(x, py, lev),
            device_id_type=MESH,
        ).wait_recv()
    for side, _, gets in sides:
        for x in others(n):

            @pl.when(gets)
            def _(side=side, x=x):
                rows = pl.ds(pl.multiple_of(x * nx, nx), nx)
                pltpu.make_async_remote_copy(
                    src_ref=halos_out.at[side, x],
                    dst_ref=halos.at[side, rows, :],
                    send_sem=halo_send.at[side, x],
                    recv_sem=halo_recv.at[side, x],
                    device_id=(x, py + (-1 if side else 1), lev),
                    device_id_type=MESH,
                ).wait_recv()

    lane = lax.broadcasted_iota(jnp.int32, (elements_x, halos.shape[2]), 1)

    def operand(k):
        parts = []
        for i in range(GLL_NODES):
            rows = pl.ds(i, elements_x, stride=GLL_NODES)
            high = rolled(halos[0, rows, :], -width * k, 1)
            low = rolled(halos[1, rows, :], width - width * k, 1)
            halo = jnp.where(lane < width, high, jnp.where(lane < 2 * width, low, 0.0))
            parts.append(jnp.concatenate([blocks[k, rows, :], halo], axis=1))
        return jnp.concatenate(parts, axis=0)

    def by_node(values):
        return [
            [
                values[i * elements_x : (i + 1) * elements_x, j * lanes : (j + 1) * lanes]
                for j in range(GLL_NODES)
            ]
            for i in range(GLL_NODES)
        ]

    tracer = by_node(
        moved_by_table(jnp.concatenate([operand(k) for k in range(held)], axis=1), spread[...])
    )
    everywhere = spread[:depth]
    for k in range(1, held):
        everywhere = everywhere + spread[k * depth : (k + 1) * depth]
    metric = moved_by_table(
        jnp.concatenate([operand(held + k) for k in range(3)], axis=0), everywhere
    )
    rows = GLL_NODES * elements_x
    node_mass, wind_x, wind_y = (by_node(metric[k * rows : (k + 1) * rows]) for k in range(3))

    slot = lax.rem(lax.broadcasted_iota(jnp.int32, (elements_x, lanes), 1), SLOTS)
    element = py * elements_y + slot - reach
    inside = (slot < elements_y + 2 * reach) & (element >= 0) & (element < nz * elements_y)
    evolved = sections(tracer, node_mass, wind_x, wind_y, inside)

    evolved = moved_by_table(
        jnp.concatenate([jnp.concatenate(row, axis=1) for row in evolved], axis=0), gather[...]
    )
    for k in range(held):
        for i in range(GLL_NODES):
            results_out[k, pl.ds(i, elements_x, stride=GLL_NODES), :] = evolved[
                i * elements_x : (i + 1) * elements_x, k * ny : (k + 1) * ny
            ]

    def result_copy(x, level, holder, to):
        return pltpu.make_async_remote_copy(
            src_ref=results_out.at[:, pl.ds(pl.multiple_of(x * nx, nx), nx), :],
            dst_ref=results.at[level, pl.ds(holder * held, held)],
            send_sem=result_send.at[x],
            recv_sem=result_recv.at[level, holder],
            device_id=to,
            device_id_type=MESH,
        )

    holder = lax.rem(px, half)
    for d, x in enumerate(others(n)):
        copy = result_copy(x, lev, holder, (x, py, target_lev))
        if d:
            copy.start()
        else:
            pl.when(target_lev != lev)(copy.start)

    @pl.when(target_lev == lev)
    def _():
        results[lev, pl.ds(holder * held, held)] = results_out[:, mine, :]

    for level in range(nlev):
        for j in range(half):
            x = lev * half + j

            @pl.when(jnp.logical_or(x != px, lev != level))
            def _(x=x, level=level, j=j):
                result_copy(px, level, j, (x, py, level)).wait_recv()

    for a in range(nlev):
        total = remap[a, 0] * results[0]
        for b in range(1, nlev):
            total = total + remap[a, b] * results[b]
        out[a] = total

    for x in others(n)[1:]:
        block_copy(x).wait_send()
    for side, sends, _ in sides:
        for x in others(n):

            @pl.when(sends)
            def _(side=side, x=x):
                halo_copy(x, side).wait_send()

    for d, x in enumerate(others(n)):
        copy = result_copy(x, lev, holder, (x, py, target_lev))
        if d:
            copy.wait_send()
        else:
            pl.when(target_lev != lev)(copy.wait_send)


def shards(n, nz, nlev, tracer, node_mass, wind_x, wind_y, remap):
    levels, tracers, nx, ny = tracer.shape
    held = tracers // n
    fields = held + 3
    reach = SECTION_REACH * len(section_weights)
    width = reach * GLL_NODES
    elements_y = ny // GLL_NODES
    if levels != 1 or tracers % n or n % nlev or nx % 8 or ny % 128:
        raise ValueError("unsupported split")
    if elements_y + 2 * reach > SLOTS or fields * width > 128 or width > ny:
        raise ValueError("unsupported block")
    lanes = -(-held * SLOTS // 128) * 128
    vmem, dma = pltpu.VMEM, pltpu.SemaphoreType.DMA
    f32 = jnp.float32
    anywhere = pl.BlockSpec(memory_space=pl.ANY)
    return pl.pallas_call(
        functools.partial(kernel, n, nz, nlev),
        out_shape=jax.ShapeDtypeStruct((nlev, tracers // nlev, nx, ny), f32),
        in_specs=[anywhere] * 4 + [pl.BlockSpec(memory_space=pltpu.SMEM)],
        out_specs=pl.BlockSpec(memory_space=pltpu.VMEM),
        scratch_shapes=[
            vmem((tracers, nx, ny), f32),
            vmem((3, nx, ny), f32),
            vmem((n, fields, nx, ny), f32),
            vmem((2, n, nx, 128), f32),
            vmem((fields, n * nx, ny), f32),
            vmem((2, n * nx, 128), f32),
            vmem((held * (ny + 128), GLL_NODES * lanes), jnp.bfloat16),
            vmem((GLL_NODES * lanes, held * ny), jnp.bfloat16),
            vmem((held, n * nx, ny), f32),
            vmem((nlev, tracers // nlev, nx, ny), f32),
            dma((4,)),
            dma((n,)),
            dma((n,)),
            dma((2, n)),
            dma((2, n)),
            dma((n,)),
            dma((nlev, n // nlev)),
        ],
        compiler_params=pltpu.CompilerParams(
            collective_id=0, has_side_effects=True, vmem_limit_bytes=32 * 1024 * 1024
        ),
        name="limited_step",
    )(tracer, node_mass, wind_x, wind_y, remap)


def solution(mesh):
    sizes = [mesh.shape[axis] for axis in ("px", "py", "lev")]
    in_specs = (
        P("lev", None, "px", "py"),
        P("lev", "px", "py"),
        P("lev", "px", "py"),
        P("lev", "px", "py"),
        P(),
    )
    out_specs = P(None, "lev", "px", "py")
    return jax.shard_map(
        functools.partial(shards, *sizes),
        mesh=mesh,
        in_specs=in_specs,
        out_specs=out_specs,
        check_vma=False,
    )
```

time: 89 us -> 16.6 us (0.19)
  starting transfers between devices: 40.6 us -> 0 us
  waiting for transfers between devices: 20.6 us -> 0 us
  Pallas kernels: 0 us -> 12.2 us
  other arithmetic: 7.71 us -> 0 us
  local copies, waits for them, and re-layouts: 11 us -> 4.11 us
  blocking collectives: 6.65 us -> 0 us
  matrix products: 1.48 us -> 0 us
    ppermute x28 -> x0, starting transfers between devices: 40.6 us -> none  [the longest x14 24.2 us: extended(): lax.ppermute(lax.slice_in_dim(block, 0, width, axis=dim), axis, backward)]
    ppermute x28 -> x0, waiting for transfers between devices: 20.6 us -> none  [the longest x14 19.6 us: extended(): lax.ppermute(lax.slice_in_dim(block, block.shape[dim] - width, None, axis...]
    pallas_call x0 -> x1, Pallas kernels: none -> 12.2 us  [shards(): pl.pallas_call(functools.partial(kernel, n, nz, nlev), out_shape=jax.Shap...]
    all_to_all x1 -> x0, blocking collectives: 6.65 us -> none  [shards(): lax.all_to_all(field, 'lev', split_axis=1, concat_axis=0, tiled=True)]
    slice x30 -> x0, local copies, waits for them, and re-layouts: 3.8 us -> none  [the longest x11 1.34 us: extended(): lax.slice_in_dim(block, block.shape[dim] - width, None, axis=dim)]
    concatenate x15 -> x0, other arithmetic: 3.15 us -> none  [the longest x8 3.08 us: pair_sum(): jnp.concatenate([head_nodes + before, middle, tail_nodes + following], ax...]
    add x11 -> x0, other arithmetic: 2.42 us -> none  [the longest x8 2.37 us: pair_sum(): head_nodes + before]
    unnamed x21 -> x11, local copies, waits for them, and re-layouts: 1.9 us -> 4.11 us
  transfers between devices with their start and end apart: 28 -> 0, of which waited for: 15 -> 0; matrix products, arithmetic and copies ran while one was open for 4% -> 0% of each run, Pallas kernels for 0% -> 0%
where the time goes in v1:
time: 16.6 us; the launch traced here: 16.3 us
  Pallas kernels  12.2 us (73%)
  local copies, waits for them, and re-layouts  4.11 us (25%)
    pallas_call x1, Pallas kernels, shards(): pl.pallas_call(functools.partial(kernel, n, nz, nlev), out_shape=jax.Shap...  12.2 us
    unnamed x11, local copies, waits for them, and re-layouts  4.11 us

profile of v1, /device:TPU:0, one launch (start us, length us, event | category | flops | bytes accessed | tf_op | source)
XLA Modules:
  0.0 16.3 jit_solution(3567049321634921361)
XLA Ops:
  0.0 0.0 copy-start
  0.0 0.8 %copy-done = f32[1,8,8,128]{3,2,1,0:T(8,128)S(1)} copy-done((f32[1,8,8,128]{3,2,1,0:T(8,128)S(1)}, f32[1,8,8,128]{3,2,1,0:T(8,128)}, u32[]{:S(2)}) %copy-start) | copy-done | bytes 32792
  0.8 0.0 copy-start.1
  0.8 0.7 %copy-done.1 = f32[1,8,128]{2,1,0:T(8,128)S(1)} copy-done((f32[1,8,128]{2,1,0:T(8,128)S(1)}, f32[1,8,128]{2,1,0:T(8,128)}, u32[]{:S(2)}) %copy-start.1) | copy-done | bytes 4120
  1.4 0.0 copy-start.2
  1.4 0.7 %copy-done.2 = f32[1,8,128]{2,1,0:T(8,128)S(1)} copy-done((f32[1,8,128]{2,1,0:T(8,128)S(1)}, f32[1,8,128]{2,1,0:T(8,128)}, u32[]{:S(2)}) %copy-start.2) | copy-done | bytes 4120
  2.1 0.0 copy-start.3
  2.1 0.7 %copy-done.3 = f32[1,8,128]{2,1,0:T(8,128)S(1)} copy-done((f32[1,8,128]{2,1,0:T(8,128)S(1)}, f32[1,8,128]{2,1,0:T(8,128)}, u32[]{:S(2)}) %copy-start.3) | copy-done | bytes 4120
  2.8 0.0 copy-start.4
  2.8 0.7 %copy-done.4 = f32[2,2]{1,0:T(2,128)S(1)} copy-done((f32[2,2]{1,0:T(2,128)S(1)}, f32[2,2]{1,0:T(2,128)}, u32[]{:S(2)}) %copy-start.4) | copy-done | bytes 40
  3.5 12.2 %limited_step.1 = f32[2,4,8,128]{3,2,1,0:T(8,128)S(1)} custom-call(f32[1,8,8,128]{3,2,1,0:T(8,128)S(1)} %copy-done, f32[1,8,128]{2,1,0:T(8,128)S(1)} %copy-done.1, f32[1,8,128]{2,1,0:T(8,128)S(1)} %copy-done.2, f32[1,8,128]{2,1,0:T(8,128)S(1)} %copy-done.3, f32[2,2]{1,0:T(2,128)S(1)} %copy-done.4), custom_call_target="tpu_custom_call" | custom-call | tf_op jit(solution)/shard_map/limited_step/pallas_call | solution.py:410
  15.7 0.6 %copy.7 = f32[2,4,8,128]{3,2,1,0:T(8,128)} copy(f32[2,4,8,128]{3,2,1,0:T(8,128)S(1)} %limited_step.1) | data formatting | bytes 65536
Async XLA Ops:
  0.0 0.8 %copy-start = (f32[1,8,8,128]{3,2,1,0:T(8,128)S(1)}, f32[1,8,8,128]{3,2,1,0:T(8,128)}, u32[]{:S(2)}) copy-start(f32[1,8,8,128]{3,2,1,0:T(8,128)} %tracer_hbm.1) | copy-start | bytes 98308
  0.8 0.7 %copy-start.1 = (f32[1,8,128]{2,1,0:T(8,128)S(1)}, f32[1,8,128]{2,1,0:T(8,128)}, u32[]{:S(2)}) copy-start(f32[1,8,128]{2,1,0:T(8,128)} %mass_hbm.1) | copy-start | bytes 12292
  1.4 0.7 %copy-start.2 = (f32[1,8,128]{2,1,0:T(8,128)S(1)}, f32[1,8,128]{2,1,0:T(8,128)}, u32[]{:S(2)}) copy-start(f32[1,8,128]{2,1,0:T(8,128)} %wind_x_hbm.1) | copy-start | bytes 12292
  2.1 0.7 %copy-start.3 = (f32[1,8,128]{2,1,0:T(8,128)S(1)}, f32[1,8,128]{2,1,0:T(8,128)}, u32[]{:S(2)}) copy-start(f32[1,8,128]{2,1,0:T(8,128)} %wind_y_hbm.1) | copy-start | bytes 12292
  2.8 0.7 %copy-start.4 = (f32[2,2]{1,0:T(2,128)S(1)}, f32[2,2]{1,0:T(2,128)}, u32[]{:S(2)}) copy-start(f32[2,2]{1,0:T(2,128)} %remap.1) | copy-start | bytes 52

commit v2 on v1

--- a/solution.py
+++ b/solution.py
@@ -123,10 +123,11 @@
     mass_hbm,
     wind_x_hbm,
     wind_y_hbm,
-    remap,
+    remap_hbm,
     out,
     tracer_in,
     metric_in,
+    remap,
     blocks_out,
     halos_out,
     blocks,
@@ -174,10 +175,13 @@
     copies = [pltpu.make_async_copy(tracer_hbm.at[0], tracer_in, in_sem.at[0])]
     for k, source in enumerate((mass_hbm, wind_x_hbm, wind_y_hbm)):
         copies.append(pltpu.make_async_copy(source.at[0], metric_in.at[k], in_sem.at[k + 1]))
+    remap_copy = pltpu.make_async_copy(remap_hbm, remap, in_sem.at[4])
+    remap_copy.start()
     for copy in copies:
         copy.start()
     for copy in copies:
         copy.wait()
+    remap_copy.wait()
 
     lane = lax.broadcasted_iota(jnp.int32, (nx, halos.shape[2]), 1)
 
@@ -406,15 +410,16 @@
     lanes = -(-held * SLOTS // 128) * 128
     vmem, dma = pltpu.VMEM, pltpu.SemaphoreType.DMA
     f32 = jnp.float32
-    anywhere = pl.BlockSpec(memory_space=pl.ANY)
+    anywhere = pl.BlockSpec(memory_space=pltpu.HBM)
     return pl.pallas_call(
         functools.partial(kernel, n, nz, nlev),
         out_shape=jax.ShapeDtypeStruct((nlev, tracers // nlev, nx, ny), f32),
-        in_specs=[anywhere] * 4 + [pl.BlockSpec(memory_space=pltpu.SMEM)],
+        in_specs=[anywhere] * 5,
         out_specs=pl.BlockSpec(memory_space=pltpu.VMEM),
         scratch_shapes=[
             vmem((tracers, nx, ny), f32),
             vmem((3, nx, ny), f32),
+            pltpu.SMEM(remap.shape, f32),
             vmem((n, fields, nx, ny), f32),
             vmem((2, n, nx, 128), f32),
             vmem((fields, n * nx, ny), f32),
@@ -423,7 +428,7 @@
             vmem((GLL_NODES * lanes, held * ny), jnp.bfloat16),
             vmem((held, n * nx, ny), f32),
             vmem((nlev, tracers // nlev, nx, ny), f32),
-            dma((4,)),
+            dma((5,)),
             dma((n,)),
             dma((n,)),
             dma((2, n)),
@@ -432,7 +437,7 @@
             dma((nlev, n // nlev)),
         ],
         compiler_params=pltpu.CompilerParams(
-            collective_id=0, has_side_effects=True, vmem_limit_bytes=32 * 1024 * 1024
+            collective_id=0, has_side_effects=True, vmem_limit_bytes=60 * 1024 * 1024
         ),
         name="limited_step",
     )(tracer, node_mass, wind_x, wind_y, remap)

time: 16.6 us -> 13.9 us (0.84)
  local copies, waits for them, and re-layouts: 4.11 us -> 1.38 us
    unnamed x11 -> x1, local copies, waits for them, and re-layouts: 4.11 us -> 1.38 us
where the time goes in v2:
time: 13.9 us; the launch traced here: 13.6 us
  Pallas kernels  12.2 us (88%)
  local copies, waits for them, and re-layouts  1.38 us (10%)
    pallas_call x1, Pallas kernels, shards(): pl.pallas_call(functools.partial(kernel, n, nz, nlev), out_shape=jax.Shap...  12.2 us
    unnamed x1, local copies, waits for them, and re-layouts  1.38 us

profile of v2, /device:TPU:0, one launch (start us, length us, event | category | flops | bytes accessed | tf_op | source)
XLA Modules:
  0.0 13.6 jit_solution(3651907007079186151)
XLA Ops:
  0.0 12.2 %limited_step.1 = f32[2,4,8,128]{3,2,1,0:T(8,128)} custom-call(f32[1,8,8,128]{3,2,1,0:T(8,128)} %tracer_hbm.1, f32[1,8,128]{2,1,0:T(8,128)} %mass_hbm.1, f32[1,8,128]{2,1,0:T(8,128)} %wind_x_hbm.1, f32[1,8,128]{2,1,0:T(8,128)} %wind_y_hbm.1, f32[2,2]{1,0:T(2,128)} %remap_hbm.1), custom_call_target="tpu_custom_call" | custom-call | tf_op jit(solution)/shard_map/limited_step/pallas_call | solution.py:414
  12.3 1.4 %copy.7 = f32[2,4,8,128]{3,2,1,0:T(8,128)} copy(f32[2,4,8,128]{3,2,1,0:T(8,128)} %limited_step.1) | data formatting | bytes 65536

commit v3 on v2

--- a/solution.py
+++ b/solution.py
@@ -181,7 +181,7 @@
         copy.start()
     for copy in copies:
         copy.wait()
-    remap_copy.wait()
+
 
     lane = lax.broadcasted_iota(jnp.int32, (nx, halos.shape[2]), 1)
 
@@ -373,6 +373,7 @@
             def _(x=x, level=level, j=j):
                 result_copy(px, level, j, (x, py, level)).wait_recv()
 
+    remap_copy.wait()
     for a in range(nlev):
         total = remap[a, 0] * results[0]
         for b in range(1, nlev):
@@ -413,7 +414,7 @@
     anywhere = pl.BlockSpec(memory_space=pltpu.HBM)
     return pl.pallas_call(
         functools.partial(kernel, n, nz, nlev),
-        out_shape=jax.ShapeDtypeStruct((nlev, tracers // nlev, nx, ny), f32),
+        out_shape=vmem((nlev, tracers // nlev, nx, ny), f32),
         in_specs=[anywhere] * 5,
         out_specs=pl.BlockSpec(memory_space=pltpu.VMEM),
         scratch_shapes=[
@@ -437,10 +438,15 @@
             dma((nlev, n // nlev)),
         ],
         compiler_params=pltpu.CompilerParams(
-            collective_id=0, has_side_effects=True, vmem_limit_bytes=60 * 1024 * 1024
+            collective_id=0, has_side_effects=True, vmem_limit_bytes=32 * 1024 * 1024
         ),
         name="limited_step",
-    )(tracer, node_mass, wind_x, wind_y, remap)
+    )(
+        *(
+            pltpu.with_memory_space_constraint(operand, pltpu.HBM)
+            for operand in (tracer, node_mass, wind_x, wind_y, remap)
+        )
+    )
 
 
 def solution(mesh):

time: 13.9 us -> 12.5 us (0.90)
  local copies, waits for them, and re-layouts: 1.38 us -> 0.62 us
  Pallas kernels: 12.2 us -> 11.7 us
    unnamed x1, local copies, waits for them, and re-layouts: 1.38 us -> 0.62 us
    pallas_call x1, Pallas kernels: 12.2 us -> 11.7 us  [shards(): pl.pallas_call(functools.partial(kernel, n, nz, nlev), out_shape=vmem((nl...]
where the time goes in v3:
time: 12.5 us; the launch traced here: 12.3 us
  Pallas kernels  11.7 us (94%)
  local copies, waits for them, and re-layouts  0.62 us (5%)
    pallas_call x1, Pallas kernels, shards(): pl.pallas_call(functools.partial(kernel, n, nz, nlev), out_shape=vmem((nl...  11.7 us
    unnamed x1, local copies, waits for them, and re-layouts  0.62 us

profile of v3, /device:TPU:0, one launch (start us, length us, event | category | flops | bytes accessed | tf_op | source)
XLA Modules:
  0.0 12.3 jit_solution(2806923835519286799)
XLA Ops:
  0.0 11.7 %limited_step.1 = f32[2,4,8,128]{3,2,1,0:T(8,128)S(1)} custom-call(f32[1,8,8,128]{3,2,1,0:T(8,128)} %tracer_hbm.1, f32[1,8,128]{2,1,0:T(8,128)} %mass_hbm.1, f32[1,8,128]{2,1,0:T(8,128)} %wind_x_hbm.1, f32[1,8,128]{2,1,0:T(8,128)} %wind_y_hbm.1, f32[2,2]{1,0:T(2,128)} %remap_hbm.1), custom_call_target="tpu_custom_call" | custom-call | tf_op jit(solution)/shard_map/limited_step/pallas_call | solution.py:415
  11.7 0.6 %copy.7 = f32[2,4,8,128]{3,2,1,0:T(8,128)} copy(f32[2,4,8,128]{3,2,1,0:T(8,128)S(1)} %limited_step.1) | data formatting | bytes 65536

commit v4 on v3

--- a/solution.py
+++ b/solution.py
@@ -49,13 +49,11 @@
 def moved_by_table(values, table):
     rows = values.shape[0]
     high = values.astype(jnp.bfloat16)
-    rest = values - high.astype(jnp.float32)
-    middle = rest.astype(jnp.bfloat16)
-    low = (rest - middle.astype(jnp.float32)).astype(jnp.bfloat16)
+    low = (values - high.astype(jnp.float32)).astype(jnp.bfloat16)
     terms = jnp.dot(
-        jnp.concatenate([high, middle, low], axis=0), table, preferred_element_type=jnp.float32
-    )
-    return terms[:rows] + (terms[rows : 2 * rows] + terms[2 * rows :])
+        jnp.concatenate([high, low], axis=0), table, preferred_element_type=jnp.float32
+    )
+    return terms[:rows] + terms[rows:]
 
 
 def sections(tracer, node_mass, wind_x, wind_y, inside):
@@ -152,25 +150,13 @@
     width = reach * GLL_NODES
     elements_y = ny // GLL_NODES
     elements_x = n * nx // GLL_NODES
-    lanes = spread.shape[1] // GLL_NODES
+    lanes = gather.shape[0] // GLL_NODES
     px, py, lev = lax.axis_index("px"), lax.axis_index("py"), lax.axis_index("lev")
     has_low, has_high = py > 0, py < nz - 1
     target_lev = px // half
 
     def others(number):
         return [lax.rem(px + d, n) for d in range(number)]
-
-    barrier = pltpu.get_barrier_semaphore()
-
-    def greet(x, y, level):
-        pl.semaphore_signal(barrier, inc=1, device_id=(x, y, level), device_id_type=MESH)
-
-    for d, x in enumerate(others(n)):
-        pl.when(has_low)(functools.partial(greet, x, py - 1, lev))
-        pl.when(has_high)(functools.partial(greet, x, py + 1, lev))
-        for step in range(nlev):
-            if d or step:
-                greet(x, py, lax.rem(lev + step, nlev))
 
     copies = [pltpu.make_async_copy(tracer_hbm.at[0], tracer_in, in_sem.at[0])]
     for k, source in enumerate((mass_hbm, wind_x_hbm, wind_y_hbm)):
@@ -179,6 +165,19 @@
     remap_copy.start()
     for copy in copies:
         copy.start()
+
+    barrier = pltpu.get_barrier_semaphore()
+
+    def greet(x, y, level):
+        pl.semaphore_signal(barrier, inc=1, device_id=(x, y, level), device_id_type=MESH)
+
+    for d, x in enumerate(others(n)):
+        pl.when(has_low)(functools.partial(greet, x, py - 1, lev))
+        pl.when(has_high)(functools.partial(greet, x, py + 1, lev))
+        for step in range(nlev):
+            if d or step:
+                greet(x, py, lax.rem(lev + step, nlev))
+
     for copy in copies:
         copy.wait()
 
@@ -228,14 +227,14 @@
         )
 
     sides = ((0, has_low, has_high), (1, has_high, has_low))
-    for x in others(n)[1:]:
-        block_copy(x).start()
     for side, sends, _ in sides:
         for x in others(n):
 
             @pl.when(sends)
             def _(side=side, x=x):
                 halo_copy(x, side).start()
+    for x in others(n)[1:]:
+        block_copy(x).start()
 
     blocks[:, mine, :] = blocks_out[px]
     for side, _, gets in sides:
@@ -252,14 +251,11 @@
     slot = jnp.where(
         source < ny + width,
         reach + source // GLL_NODES,
-        jnp.where(source < ny + 2 * width, (source - ny - width) // GLL_NODES, -SLOTS * lanes),
-    )
-    place = lax.rem(source, GLL_NODES) * lanes + slot
+        jnp.where(source < ny + 2 * width, (source - ny - width) // GLL_NODES, -SLOTS * GLL_NODES),
+    )
+    place = lax.rem(source, GLL_NODES) * SLOTS + slot
     column = node_of((1, spread.shape[1]), 1)
-    for k in range(held):
-        spread[k * depth : (k + 1) * depth] = jnp.where(
-            place + k * SLOTS == column, 1.0, 0.0
-        ).astype(jnp.bfloat16)
+    spread[...] = jnp.where(place == column, 1.0, 0.0).astype(jnp.bfloat16)
     source = node_of((gather.shape[0], 1), 0)
     at = lax.rem(source, lanes)
     element = lax.rem(at, SLOTS) - reach
@@ -271,16 +267,6 @@
         jnp.bfloat16
     )
 
-    for x in others(n)[1:]:
-        rows = pl.ds(pl.multiple_of(x * nx, nx), nx)
-        pltpu.make_async_remote_copy(
-            src_ref=blocks_out.at[x],
-            dst_ref=blocks.at[:, rows, :],
-            send_sem=block_send.at[x],
-            recv_sem=block_recv.at[x],
-            device_id=(x, py, lev),
-            device_id_type=MESH,
-        ).wait_recv()
     for side, _, gets in sides:
         for x in others(n):
 
@@ -297,37 +283,68 @@
                 ).wait_recv()
 
     lane = lax.broadcasted_iota(jnp.int32, (elements_x, halos.shape[2]), 1)
-
-    def operand(k):
-        parts = []
-        for i in range(GLL_NODES):
-            rows = pl.ds(i, elements_x, stride=GLL_NODES)
-            high = rolled(halos[0, rows, :], -width * k, 1)
-            low = rolled(halos[1, rows, :], width - width * k, 1)
-            halo = jnp.where(lane < width, high, jnp.where(lane < 2 * width, low, 0.0))
-            parts.append(jnp.concatenate([blocks[k, rows, :], halo], axis=1))
-        return jnp.concatenate(parts, axis=0)
-
-    def by_node(values):
+    rows_of = [pl.ds(i, elements_x, stride=GLL_NODES) for i in range(GLL_NODES)]
+    rims = []
+    for rows in rows_of:
+        high, low = halos[0, rows, :], halos[1, rows, :]
+        rims.append(
+            [
+                jnp.where(
+                    lane < width,
+                    rolled(high, -width * k, 1),
+                    jnp.where(lane < 2 * width, rolled(low, width - width * k, 1), 0.0),
+                )
+                for k in range(fields)
+            ]
+        )
+
+    for x in others(n)[1:]:
+        rows = pl.ds(pl.multiple_of(x * nx, nx), nx)
+        pltpu.make_async_remote_copy(
+            src_ref=blocks_out.at[x],
+            dst_ref=blocks.at[:, rows, :],
+            send_sem=block_send.at[x],
+            recv_sem=block_recv.at[x],
+            device_id=(x, py, lev),
+            device_id_type=MESH,
+        ).wait_recv()
+
+    parts = [
+        jnp.concatenate([blocks[k, rows_of[i], :], rims[i][k]], axis=1)
+        for k in range(fields)
+        for i in range(GLL_NODES)
+    ]
+    spread_out = moved_by_table(jnp.concatenate(parts, axis=0), spread[...])
+    pair = 2 * SLOTS
+    in_first = lax.broadcasted_iota(jnp.int32, (elements_x, pair), 1) < SLOTS
+
+    def joined(first, second, i, j):
+        first, second = (
+            spread_out[
+                (k * GLL_NODES + i) * elements_x : (k * GLL_NODES + i + 1) * elements_x,
+                j // 2 * pair : (j // 2 + 1) * pair,
+            ]
+            for k in (first, second)
+        )
+        if j % 2:
+            first = rolled(first, SLOTS, 1)
+        else:
+            second = rolled(second, SLOTS, 1)
+        return jnp.where(in_first, first, second)
+
+    def by_node(pairs):
         return [
             [
-                values[i * elements_x : (i + 1) * elements_x, j * lanes : (j + 1) * lanes]
+                jnp.concatenate([joined(first, second, i, j) for first, second in pairs], axis=1)
                 for j in range(GLL_NODES)
             ]
             for i in range(GLL_NODES)
         ]
 
-    tracer = by_node(
-        moved_by_table(jnp.concatenate([operand(k) for k in range(held)], axis=1), spread[...])
-    )
-    everywhere = spread[:depth]
-    for k in range(1, held):
-        everywhere = everywhere + spread[k * depth : (k + 1) * depth]
-    metric = moved_by_table(
-        jnp.concatenate([operand(held + k) for k in range(3)], axis=0), everywhere
-    )
-    rows = GLL_NODES * elements_x
-    node_mass, wind_x, wind_y = (by_node(metric[k * rows : (k + 1) * rows]) for k in range(3))
+    tracer = by_node([(k, min(k + 1, held - 1)) for k in range(0, held, 2)])
+    node_mass, wind_x, wind_y = (
+        by_node([(held + k, held + k)] * (lanes // pair)) for k in range(3)
+    )
 
     slot = lax.rem(lax.broadcasted_iota(jnp.int32, (elements_x, lanes), 1), SLOTS)
     element = py * elements_y + slot - reach
@@ -425,7 +442,7 @@
             vmem((2, n, nx, 128), f32),
             vmem((fields, n * nx, ny), f32),
             vmem((2, n * nx, 128), f32),
-            vmem((held * (ny + 128), GLL_NODES * lanes), jnp.bfloat16),
+            vmem((ny + 128, GLL_NODES * SLOTS), jnp.bfloat16),
             vmem((GLL_NODES * lanes, held * ny), jnp.bfloat16),
             vmem((held, n * nx, ny), f32),
             vmem((nlev, tracers // nlev, nx, ny), f32),

time: 12.5 us -> 12.5 us (level)
  no operation moved by 1% of the time
where the time goes in v4:
time: 12.5 us; the launch traced here: 12.4 us
  Pallas kernels  11.7 us (94%)
  local copies, waits for them, and re-layouts  0.62 us (5%)
    pallas_call x1, Pallas kernels, shards(): pl.pallas_call(functools.partial(kernel, n, nz, nlev), out_shape=vmem((nl...  11.7 us
    unnamed x1, local copies, waits for them, and re-layouts  0.62 us

profile of v4, /device:TPU:0, one launch (start us, length us, event | category | flops | bytes accessed | tf_op | source)
XLA Modules:
  0.0 12.4 jit_solution(16023609948248631174)
XLA Ops:
  0.0 11.7 %limited_step.1 = f32[2,4,8,128]{3,2,1,0:T(8,128)S(1)} custom-call(f32[1,8,8,128]{3,2,1,0:T(8,128)} %tracer_hbm.1, f32[1,8,128]{2,1,0:T(8,128)} %mass_hbm.1, f32[1,8,128]{2,1,0:T(8,128)} %wind_x_hbm.1, f32[1,8,128]{2,1,0:T(8,128)} %wind_y_hbm.1, f32[2,2]{1,0:T(2,128)} %remap_hbm.1), custom_call_target="tpu_custom_call" | custom-call | tf_op jit(solution)/shard_map/limited_step/pallas_call | solution.py:432
  11.8 0.6 %copy.7 = f32[2,4,8,128]{3,2,1,0:T(8,128)} copy(f32[2,4,8,128]{3,2,1,0:T(8,128)S(1)} %limited_step.1) | data formatting | bytes 65536

commit v5 on v4

--- a/solution.py
+++ b/solution.py
@@ -155,8 +155,13 @@
     has_low, has_high = py > 0, py < nz - 1
     target_lev = px // half
 
-    def others(number):
-        return [lax.rem(px + d, n) for d in range(number)]
+    def others():
+        return [lax.rem(px + d, n) for d in sorted(range(1, n), key=lambda d: abs(2 * d - n))]
+
+    everyone = others() + [px]
+
+    def took(ref, sem):
+        pltpu.make_async_copy(ref, ref, sem).wait()
 
     copies = [pltpu.make_async_copy(tracer_hbm.at[0], tracer_in, in_sem.at[0])]
     for k, source in enumerate((mass_hbm, wind_x_hbm, wind_y_hbm)):
@@ -171,12 +176,18 @@
     def greet(x, y, level):
         pl.semaphore_signal(barrier, inc=1, device_id=(x, y, level), device_id_type=MESH)
 
-    for d, x in enumerate(others(n)):
-        pl.when(has_low)(functools.partial(greet, x, py - 1, lev))
-        pl.when(has_high)(functools.partial(greet, x, py + 1, lev))
-        for step in range(nlev):
-            if d or step:
-                greet(x, py, lax.rem(lev + step, nlev))
+    for near, there in ((has_low, py - 1), (has_high, py + 1)):
+
+        @pl.when(near)
+        def _(there=there):
+            for x in everyone:
+                greet(x, there, lev)
+
+    for x in everyone:
+        for step in range(1, nlev):
+            greet(x, py, lax.rem(lev + step, nlev))
+    for x in others():
+        greet(x, py, lev)
 
     for copy in copies:
         copy.wait()
@@ -210,8 +221,8 @@
         return pltpu.make_async_remote_copy(
             src_ref=blocks_out.at[x],
             dst_ref=blocks.at[:, mine, :],
-            send_sem=block_send.at[x],
-            recv_sem=block_recv.at[px],
+            send_sem=block_send,
+            recv_sem=block_recv,
             device_id=(x, py, lev),
             device_id_type=MESH,
         )
@@ -220,21 +231,21 @@
         return pltpu.make_async_remote_copy(
             src_ref=halos_out.at[side, x],
             dst_ref=halos.at[side, mine, :],
-            send_sem=halo_send.at[side, x],
-            recv_sem=halo_recv.at[side, px],
+            send_sem=halo_send.at[side],
+            recv_sem=halo_recv.at[side],
             device_id=(x, py + (1 if side else -1), lev),
             device_id_type=MESH,
         )
 
     sides = ((0, has_low, has_high), (1, has_high, has_low))
+    for x in others():
+        block_copy(x).start()
     for side, sends, _ in sides:
-        for x in others(n):
-
-            @pl.when(sends)
-            def _(side=side, x=x):
+
+        @pl.when(sends)
+        def _(side=side):
+            for x in everyone:
                 halo_copy(x, side).start()
-    for x in others(n)[1:]:
-        block_copy(x).start()
 
     blocks[:, mine, :] = blocks_out[px]
     for side, _, gets in sides:
@@ -268,19 +279,10 @@
     )
 
     for side, _, gets in sides:
-        for x in others(n):
-
-            @pl.when(gets)
-            def _(side=side, x=x):
-                rows = pl.ds(pl.multiple_of(x * nx, nx), nx)
-                pltpu.make_async_remote_copy(
-                    src_ref=halos_out.at[side, x],
-                    dst_ref=halos.at[side, rows, :],
-                    send_sem=halo_send.at[side, x],
-                    recv_sem=halo_recv.at[side, x],
-                    device_id=(x, py + (-1 if side else 1), lev),
-                    device_id_type=MESH,
-                ).wait_recv()
+
+        @pl.when(gets)
+        def _(side=side):
+            took(halos.at[side], halo_recv.at[side])
 
     lane = lax.broadcasted_iota(jnp.int32, (elements_x, halos.shape[2]), 1)
     rows_of = [pl.ds(i, elements_x, stride=GLL_NODES) for i in range(GLL_NODES)]
@@ -298,16 +300,7 @@
             ]
         )
 
-    for x in others(n)[1:]:
-        rows = pl.ds(pl.multiple_of(x * nx, nx), nx)
-        pltpu.make_async_remote_copy(
-            src_ref=blocks_out.at[x],
-            dst_ref=blocks.at[:, rows, :],
-            send_sem=block_send.at[x],
-            recv_sem=block_recv.at[x],
-            device_id=(x, py, lev),
-            device_id_type=MESH,
-        ).wait_recv()
+    took(blocks.at[:, : (n - 1) * nx, :], block_recv)
 
     parts = [
         jnp.concatenate([blocks[k, rows_of[i], :], rims[i][k]], axis=1)
@@ -360,35 +353,31 @@
                 i * elements_x : (i + 1) * elements_x, k * ny : (k + 1) * ny
             ]
 
-    def result_copy(x, level, holder, to):
+    holder = lax.rem(px, half)
+    is_mine = target_lev == lev
+
+    def result_copy(x):
         return pltpu.make_async_remote_copy(
             src_ref=results_out.at[:, pl.ds(pl.multiple_of(x * nx, nx), nx), :],
-            dst_ref=results.at[level, pl.ds(holder * held, held)],
-            send_sem=result_send.at[x],
-            recv_sem=result_recv.at[level, holder],
-            device_id=to,
+            dst_ref=results.at[lev, pl.ds(holder * held, held)],
+            send_sem=result_send,
+            recv_sem=result_recv,
+            device_id=(x, py, target_lev),
             device_id_type=MESH,
         )
 
-    holder = lax.rem(px, half)
-    for d, x in enumerate(others(n)):
-        copy = result_copy(x, lev, holder, (x, py, target_lev))
-        if d:
-            copy.start()
-        else:
-            pl.when(target_lev != lev)(copy.start)
-
-    @pl.when(target_lev == lev)
+    for x in others():
+        result_copy(x).start()
+
+    @pl.when(jnp.logical_not(is_mine))
+    def _():
+        result_copy(px).start()
+        took(results_out, result_recv)
+
+    @pl.when(is_mine)
     def _():
         results[lev, pl.ds(holder * held, held)] = results_out[:, mine, :]
-
-    for level in range(nlev):
-        for j in range(half):
-            x = lev * half + j
-
-            @pl.when(jnp.logical_or(x != px, lev != level))
-            def _(x=x, level=level, j=j):
-                result_copy(px, level, j, (x, py, level)).wait_recv()
+        took(results_out.at[:, : (n - 1) * nx, :], result_recv)
 
     remap_copy.wait()
     for a in range(nlev):
@@ -397,21 +386,20 @@
             total = total + remap[a, b] * results[b]
         out[a] = total
 
-    for x in others(n)[1:]:
-        block_copy(x).wait_send()
+    took(blocks.at[:, : (n - 1) * nx, :], block_send)
     for side, sends, _ in sides:
-        for x in others(n):
-
-            @pl.when(sends)
-            def _(side=side, x=x):
-                halo_copy(x, side).wait_send()
-
-    for d, x in enumerate(others(n)):
-        copy = result_copy(x, lev, holder, (x, py, target_lev))
-        if d:
-            copy.wait_send()
-        else:
-            pl.when(target_lev != lev)(copy.wait_send)
+
+        @pl.when(sends)
+        def _(side=side):
+            took(halos.at[side], halo_send.at[side])
+
+    @pl.when(is_mine)
+    def _():
+        took(results_out.at[:, : (n - 1) * nx, :], result_send)
+
+    @pl.when(jnp.logical_not(is_mine))
+    def _():
+        took(results_out, result_send)
 
 
 def shards(n, nz, nlev, tracer, node_mass, wind_x, wind_y, remap):
@@ -447,12 +435,12 @@
             vmem((held, n * nx, ny), f32),
             vmem((nlev, tracers // nlev, nx, ny), f32),
             dma((5,)),
-            dma((n,)),
-            dma((n,)),
-            dma((2, n)),
-            dma((2, n)),
-            dma((n,)),
-            dma((nlev, n // nlev)),
+            dma,
+            dma,
+            dma((2,)),
+            dma((2,)),
+            dma,
+            dma,
         ],
         compiler_params=pltpu.CompilerParams(
             collective_id=0, has_side_effects=True, vmem_limit_bytes=32 * 1024 * 1024

time: 12.5 us -> 12.6 us (level)
  no operation moved by 1% of the time
where the time goes in v5:
time: 12.6 us; the launch traced here: 12.4 us
  Pallas kernels  11.8 us (94%)
  local copies, waits for them, and re-layouts  0.62 us (5%)
    pallas_call x1, Pallas kernels, shards(): pl.pallas_call(functools.partial(kernel, n, nz, nlev), out_shape=vmem((nl...  11.8 us
    unnamed x1, local copies, waits for them, and re-layouts  0.62 us

profile of v5, /device:TPU:0, one launch (start us, length us, event | category | flops | bytes accessed | tf_op | source)
XLA Modules:
  0.0 12.4 jit_solution(6198361760058253851)
XLA Ops:
  0.0 11.8 %limited_step.1 = f32[2,4,8,128]{3,2,1,0:T(8,128)S(1)} custom-call(f32[1,8,8,128]{3,2,1,0:T(8,128)} %tracer_hbm.1, f32[1,8,128]{2,1,0:T(8,128)} %mass_hbm.1, f32[1,8,128]{2,1,0:T(8,128)} %wind_x_hbm.1, f32[1,8,128]{2,1,0:T(8,128)} %wind_y_hbm.1, f32[2,2]{1,0:T(2,128)} %remap_hbm.1), custom_call_target="tpu_custom_call" | custom-call | tf_op jit(solution)/shard_map/limited_step/pallas_call | solution.py:420
  11.8 0.6 %copy.7 = f32[2,4,8,128]{3,2,1,0:T(8,128)} copy(f32[2,4,8,128]{3,2,1,0:T(8,128)S(1)} %limited_step.1) | data formatting | bytes 65536

commit v6 on v5

--- a/solution.py
+++ b/solution.py
@@ -126,7 +126,6 @@
     tracer_in,
     metric_in,
     remap,
-    blocks_out,
     halos_out,
     blocks,
     halos,
@@ -163,6 +162,24 @@
     def took(ref, sem):
         pltpu.make_async_copy(ref, ref, sem).wait()
 
+    barrier = pltpu.get_barrier_semaphore()
+
+    def greet(x, y, level):
+        pl.semaphore_signal(barrier, inc=1, device_id=(x, y, level), device_id_type=MESH)
+
+    for near, there in ((has_low, py - 1), (has_high, py + 1)):
+
+        @pl.when(near)
+        def _(there=there):
+            for x in everyone:
+                greet(x, there, lev)
+
+    for x in others():
+        greet(x, py, lev)
+    for x in everyone:
+        for step in range(1, nlev):
+            greet(x, py, lax.rem(lev + step, nlev))
+
     copies = [pltpu.make_async_copy(tracer_hbm.at[0], tracer_in, in_sem.at[0])]
     for k, source in enumerate((mass_hbm, wind_x_hbm, wind_y_hbm)):
         copies.append(pltpu.make_async_copy(source.at[0], metric_in.at[k], in_sem.at[k + 1]))
@@ -170,25 +187,6 @@
     remap_copy.start()
     for copy in copies:
         copy.start()
-
-    barrier = pltpu.get_barrier_semaphore()
-
-    def greet(x, y, level):
-        pl.semaphore_signal(barrier, inc=1, device_id=(x, y, level), device_id_type=MESH)
-
-    for near, there in ((has_low, py - 1), (has_high, py + 1)):
-
-        @pl.when(near)
-        def _(there=there):
-            for x in everyone:
-                greet(x, there, lev)
-
-    for x in everyone:
-        for step in range(1, nlev):
-            greet(x, py, lax.rem(lev + step, nlev))
-    for x in others():
-        greet(x, py, lev)
-
     for copy in copies:
         copy.wait()
 
@@ -205,8 +203,6 @@
         return tile
 
     for group in range(n):
-        blocks_out[group, :held] = tracer_in[group * held : (group + 1) * held]
-        blocks_out[group, held:] = metric_in[...]
         for side in range(2):
             halos_out[side, group] = halo_tile(group, side)
 
@@ -217,15 +213,22 @@
 
     mine = pl.ds(pl.multiple_of(px * nx, nx), nx)
 
-    def block_copy(x):
-        return pltpu.make_async_remote_copy(
-            src_ref=blocks_out.at[x],
-            dst_ref=blocks.at[:, mine, :],
-            send_sem=block_send,
-            recv_sem=block_recv,
-            device_id=(x, py, lev),
-            device_id_type=MESH,
-        )
+    def block_copies(x):
+        pieces = (
+            (tracer_in.at[pl.ds(x * held, held)], blocks.at[:held, mine, :]),
+            (metric_in, blocks.at[held:, mine, :]),
+        )
+        return [
+            pltpu.make_async_remote_copy(
+                src_ref=source,
+                dst_ref=target,
+                send_sem=block_send,
+                recv_sem=block_recv,
+                device_id=(x, py, lev),
+                device_id_type=MESH,
+            )
+            for source, target in pieces
+        ]
 
     def halo_copy(x, side):
         return pltpu.make_async_remote_copy(
@@ -239,7 +242,8 @@
 
     sides = ((0, has_low, has_high), (1, has_high, has_low))
     for x in others():
-        block_copy(x).start()
+        for copy in block_copies(x):
+            copy.start()
     for side, sends, _ in sides:
 
         @pl.when(sends)
@@ -247,7 +251,8 @@
             for x in everyone:
                 halo_copy(x, side).start()
 
-    blocks[:, mine, :] = blocks_out[px]
+    blocks[:held, mine, :] = tracer_in[pl.ds(px * held, held)]
+    blocks[held:, mine, :] = metric_in[...]
     for side, _, gets in sides:
 
         @pl.when(jnp.logical_not(gets))
@@ -426,7 +431,6 @@
             vmem((tracers, nx, ny), f32),
             vmem((3, nx, ny), f32),
             pltpu.SMEM(remap.shape, f32),
-            vmem((n, fields, nx, ny), f32),
             vmem((2, n, nx, 128), f32),
             vmem((fields, n * nx, ny), f32),
             vmem((2, n * nx, 128), f32),

time: 12.6 us -> 12.6 us (level)
  no operation moved by 1% of the time
where the time goes in v6:
time: 12.6 us; the launch traced here: 12.4 us
  Pallas kernels  11.8 us (94%)
  local copies, waits for them, and re-layouts  0.62 us (5%)
    pallas_call x1, Pallas kernels, shards(): pl.pallas_call(functools.partial(kernel, n, nz, nlev), out_shape=vmem((nl...  11.8 us
    unnamed x1, local copies, waits for them, and re-layouts  0.62 us

profile of v6, /device:TPU:0, one launch (start us, length us, event | category | flops | bytes accessed | tf_op | source)
XLA Modules:
  0.0 12.4 jit_solution(14964472666738798530)
XLA Ops:
  0.0 11.8 %limited_step.1 = f32[2,4,8,128]{3,2,1,0:T(8,128)S(1)} custom-call(f32[1,8,8,128]{3,2,1,0:T(8,128)} %tracer_hbm.1, f32[1,8,128]{2,1,0:T(8,128)} %mass_hbm.1, f32[1,8,128]{2,1,0:T(8,128)} %wind_x_hbm.1, f32[1,8,128]{2,1,0:T(8,128)} %wind_y_hbm.1, f32[2,2]{1,0:T(2,128)} %remap_hbm.1), custom_call_target="tpu_custom_call" | custom-call | tf_op jit(solution)/shard_map/limited_step/pallas_call | solution.py:425
  11.8 0.6 %copy.7 = f32[2,4,8,128]{3,2,1,0:T(8,128)} copy(f32[2,4,8,128]{3,2,1,0:T(8,128)S(1)} %limited_step.1) | data formatting | bytes 65536

commit v7 on v6

--- a/solution.py
+++ b/solution.py
@@ -140,6 +140,7 @@
     halo_recv,
     result_send,
     result_recv,
+    ready,
 ):
     tracers, nx, ny = tracer_in.shape
     held = tracers // n
@@ -155,9 +156,9 @@
     target_lev = px // half
 
     def others():
-        return [lax.rem(px + d, n) for d in sorted(range(1, n), key=lambda d: abs(2 * d - n))]
-
-    everyone = others() + [px]
+        return [d + (d >= px).astype(jnp.int32) for d in range(n - 1)]
+
+    everyone = list(range(n))
 
     def took(ref, sem):
         pltpu.make_async_copy(ref, ref, sem).wait()
@@ -167,12 +168,10 @@
     def greet(x, y, level):
         pl.semaphore_signal(barrier, inc=1, device_id=(x, y, level), device_id_type=MESH)
 
-    for near, there in ((has_low, py - 1), (has_high, py + 1)):
-
-        @pl.when(near)
-        def _(there=there):
-            for x in everyone:
-                greet(x, there, lev)
+    @pl.when(has_high)
+    def _():
+        for x in everyone:
+            greet(x, py + 1, lev)
 
     for x in others():
         greet(x, py, lev)
@@ -207,9 +206,7 @@
             halos_out[side, group] = halo_tile(group, side)
 
     peers = n * nlev - 1
-    pl.semaphore_wait(
-        barrier, peers + n * (has_low.astype(jnp.int32) + has_high.astype(jnp.int32))
-    )
+    pl.semaphore_wait(barrier, peers + n * has_low.astype(jnp.int32))
 
     mine = pl.ds(pl.multiple_of(px * nx, nx), nx)
 
@@ -241,15 +238,21 @@
         )
 
     sides = ((0, has_low, has_high), (1, has_high, has_low))
+    @pl.when(has_low)
+    def _():
+        for x in everyone:
+            halo_copy(x, 0).start()
+
     for x in others():
         for copy in block_copies(x):
             copy.start()
-    for side, sends, _ in sides:
-
-        @pl.when(sends)
-        def _(side=side):
-            for x in everyone:
-                halo_copy(x, side).start()
+
+    @pl.when(has_low)
+    def _():
+        for x in everyone:
+            pl.semaphore_signal(
+                ready, inc=1, device_id=(x, py - 1, lev), device_id_type=MESH
+            )
 
     blocks[:held, mine, :] = tracer_in[pl.ds(px * held, held)]
     blocks[held:, mine, :] = metric_in[...]
@@ -282,6 +285,12 @@
     gather[...] = jnp.where(place == node_of((1, gather.shape[1]), 1), 1.0, 0.0).astype(
         jnp.bfloat16
     )
+
+    @pl.when(has_high)
+    def _():
+        pl.semaphore_wait(ready, n)
+        for x in everyone:
+            halo_copy(x, 1).start()
 
     for side, _, gets in sides:
 
@@ -371,16 +380,16 @@
             device_id_type=MESH,
         )
 
-    for x in others():
-        result_copy(x).start()
-
     @pl.when(jnp.logical_not(is_mine))
     def _():
-        result_copy(px).start()
+        for x in everyone:
+            result_copy(x).start()
         took(results_out, result_recv)
 
     @pl.when(is_mine)
     def _():
+        for x in others():
+            result_copy(x).start()
         results[lev, pl.ds(holder * held, held)] = results_out[:, mine, :]
         took(results_out.at[:, : (n - 1) * nx, :], result_recv)
 
@@ -445,6 +454,7 @@
             dma((2,)),
             dma,
             dma,
+            pltpu.SemaphoreType.REGULAR,
         ],
         compiler_params=pltpu.CompilerParams(
             collective_id=0, has_side_effects=True, vmem_limit_bytes=32 * 1024 * 1024

time: 12.6 us -> 11.5 us (0.913)
  Pallas kernels: 11.8 us -> 10.7 us
    pallas_call x1, Pallas kernels: 11.8 us -> 10.7 us  [shards(): pl.pallas_call(functools.partial(kernel, n, nz, nlev), out_shape=vmem((nl...]
where the time goes in v7:
time: 11.5 us; the launch traced here: 11.4 us
  Pallas kernels  10.7 us (93%)
  local copies, waits for them, and re-layouts  0.62 us (5%)
    pallas_call x1, Pallas kernels, shards(): pl.pallas_call(functools.partial(kernel, n, nz, nlev), out_shape=vmem((nl...  10.7 us
    unnamed x1, local copies, waits for them, and re-layouts  0.62 us

profile of v7, /device:TPU:0, one launch (start us, length us, event | category | flops | bytes accessed | tf_op | source)
XLA Modules:
  0.0 11.4 jit_solution(11799106418682733436)
XLA Ops:
  0.0 10.7 %limited_step.1 = f32[2,4,8,128]{3,2,1,0:T(8,128)S(1)} custom-call(f32[1,8,8,128]{3,2,1,0:T(8,128)} %tracer_hbm.1, f32[1,8,128]{2,1,0:T(8,128)} %mass_hbm.1, f32[1,8,128]{2,1,0:T(8,128)} %wind_x_hbm.1, f32[1,8,128]{2,1,0:T(8,128)} %wind_y_hbm.1, f32[2,2]{1,0:T(2,128)} %remap_hbm.1), custom_call_target="tpu_custom_call" | custom-call | tf_op jit(solution)/shard_map/limited_step/pallas_call | solution.py:434
  10.7 0.6 %copy.7 = f32[2,4,8,128]{3,2,1,0:T(8,128)} copy(f32[2,4,8,128]{3,2,1,0:T(8,128)S(1)} %limited_step.1) | data formatting | bytes 65536

commit v8 on v7

--- a/solution.py
+++ b/solution.py
@@ -186,9 +186,19 @@
     remap_copy.start()
     for copy in copies:
         copy.start()
+
+    peers = n * nlev - 1
+    pl.semaphore_wait(barrier, peers + n * has_low.astype(jnp.int32))
+
+    @pl.when(has_low)
+    def _():
+        for x in everyone:
+            pl.semaphore_signal(
+                ready, inc=1, device_id=(x, py - 1, lev), device_id_type=MESH
+            )
+
     for copy in copies:
         copy.wait()
-
 
     lane = lax.broadcasted_iota(jnp.int32, (nx, halos.shape[2]), 1)
 
@@ -202,11 +212,7 @@
         return tile
 
     for group in range(n):
-        for side in range(2):
-            halos_out[side, group] = halo_tile(group, side)
-
-    peers = n * nlev - 1
-    pl.semaphore_wait(barrier, peers + n * has_low.astype(jnp.int32))
+        halos_out[0, group] = halo_tile(group, 0)
 
     mine = pl.ds(pl.multiple_of(px * nx, nx), nx)
 
@@ -238,6 +244,7 @@
         )
 
     sides = ((0, has_low, has_high), (1, has_high, has_low))
+
     @pl.when(has_low)
     def _():
         for x in everyone:
@@ -247,12 +254,14 @@
         for copy in block_copies(x):
             copy.start()
 
-    @pl.when(has_low)
-    def _():
+    for group in range(n):
+        halos_out[1, group] = halo_tile(group, 1)
+
+    @pl.when(has_high)
+    def _():
+        pl.semaphore_wait(ready, n)
         for x in everyone:
-            pl.semaphore_signal(
-                ready, inc=1, device_id=(x, py - 1, lev), device_id_type=MESH
-            )
+            halo_copy(x, 1).start()
 
     blocks[:held, mine, :] = tracer_in[pl.ds(px * held, held)]
     blocks[held:, mine, :] = metric_in[...]
@@ -285,12 +294,6 @@
     gather[...] = jnp.where(place == node_of((1, gather.shape[1]), 1), 1.0, 0.0).astype(
         jnp.bfloat16
     )
-
-    @pl.when(has_high)
-    def _():
-        pl.semaphore_wait(ready, n)
-        for x in everyone:
-            halo_copy(x, 1).start()
 
     for side, _, gets in sides:
 

time: 11.5 us -> 11.5 us (level)
  no operation moved by 1% of the time
where the time goes in v8:
time: 11.5 us; the launch traced here: 11.3 us
  Pallas kernels  10.7 us (93%)
  local copies, waits for them, and re-layouts  0.62 us (5%)
    pallas_call x1, Pallas kernels, shards(): pl.pallas_call(functools.partial(kernel, n, nz, nlev), out_shape=vmem((nl...  10.7 us
    unnamed x1, local copies, waits for them, and re-layouts  0.62 us

profile of v8, /device:TPU:0, one launch (start us, length us, event | category | flops | bytes accessed | tf_op | source)
XLA Modules:
  0.0 11.3 jit_solution(15961040109382101905)
XLA Ops:
  0.0 10.7 %limited_step.1 = f32[2,4,8,128]{3,2,1,0:T(8,128)S(1)} custom-call(f32[1,8,8,128]{3,2,1,0:T(8,128)} %tracer_hbm.1, f32[1,8,128]{2,1,0:T(8,128)} %mass_hbm.1, f32[1,8,128]{2,1,0:T(8,128)} %wind_x_hbm.1, f32[1,8,128]{2,1,0:T(8,128)} %wind_y_hbm.1, f32[2,2]{1,0:T(2,128)} %remap_hbm.1), custom_call_target="tpu_custom_call" | custom-call | tf_op jit(solution)/shard_map/limited_step/pallas_call | solution.py:437
  10.7 0.6 %copy.7 = f32[2,4,8,128]{3,2,1,0:T(8,128)} copy(f32[2,4,8,128]{3,2,1,0:T(8,128)S(1)} %limited_step.1) | data formatting | bytes 65536

commit v9 on v8

--- a/solution.py
+++ b/solution.py
@@ -163,15 +163,17 @@
     def took(ref, sem):
         pltpu.make_async_copy(ref, ref, sem).wait()
 
+    copies = [pltpu.make_async_copy(tracer_hbm.at[0], tracer_in, in_sem.at[0])]
+    for k, source in enumerate((mass_hbm, wind_x_hbm, wind_y_hbm)):
+        copies.append(pltpu.make_async_copy(source.at[0], metric_in.at[k], in_sem.at[k + 1]))
+    remap_copy = pltpu.make_async_copy(remap_hbm, remap, in_sem.at[4])
+    for copy in copies:
+        copy.start()
+
     barrier = pltpu.get_barrier_semaphore()
 
     def greet(x, y, level):
         pl.semaphore_signal(barrier, inc=1, device_id=(x, y, level), device_id_type=MESH)
-
-    @pl.when(has_high)
-    def _():
-        for x in everyone:
-            greet(x, py + 1, lev)
 
     for x in others():
         greet(x, py, lev)
@@ -179,13 +181,10 @@
         for step in range(1, nlev):
             greet(x, py, lax.rem(lev + step, nlev))
 
-    copies = [pltpu.make_async_copy(tracer_hbm.at[0], tracer_in, in_sem.at[0])]
-    for k, source in enumerate((mass_hbm, wind_x_hbm, wind_y_hbm)):
-        copies.append(pltpu.make_async_copy(source.at[0], metric_in.at[k], in_sem.at[k + 1]))
-    remap_copy = pltpu.make_async_copy(remap_hbm, remap, in_sem.at[4])
-    remap_copy.start()
-    for copy in copies:
-        copy.start()
+    @pl.when(has_high)
+    def _():
+        for x in everyone:
+            greet(x, py + 1, lev)
 
     peers = n * nlev - 1
     pl.semaphore_wait(barrier, peers + n * has_low.astype(jnp.int32))
@@ -197,6 +196,7 @@
                 ready, inc=1, device_id=(x, py - 1, lev), device_id_type=MESH
             )
 
+    remap_copy.start()
     for copy in copies:
         copy.wait()
 

time: 11.5 us -> 11.5 us (level)
  no operation moved by 1% of the time
where the time goes in v9:
time: 11.5 us; the launch traced here: 11.3 us
  Pallas kernels  10.7 us (93%)
  local copies, waits for them, and re-layouts  0.62 us (5%)
    pallas_call x1, Pallas kernels, shards(): pl.pallas_call(functools.partial(kernel, n, nz, nlev), out_shape=vmem((nl...  10.7 us
    unnamed x1, local copies, waits for them, and re-layouts  0.62 us

profile of v9, /device:TPU:0, one launch (start us, length us, event | category | flops | bytes accessed | tf_op | source)
XLA Modules:
  0.0 11.3 jit_solution(15137051026460492694)
XLA Ops:
  0.0 10.7 %limited_step.1 = f32[2,4,8,128]{3,2,1,0:T(8,128)S(1)} custom-call(f32[1,8,8,128]{3,2,1,0:T(8,128)} %tracer_hbm.1, f32[1,8,128]{2,1,0:T(8,128)} %mass_hbm.1, f32[1,8,128]{2,1,0:T(8,128)} %wind_x_hbm.1, f32[1,8,128]{2,1,0:T(8,128)} %wind_y_hbm.1, f32[2,2]{1,0:T(2,128)} %remap_hbm.1), custom_call_target="tpu_custom_call" | custom-call | tf_op jit(solution)/shard_map/limited_step/pallas_call | solution.py:437
  10.7 0.6 %copy.7 = f32[2,4,8,128]{3,2,1,0:T(8,128)} copy(f32[2,4,8,128]{3,2,1,0:T(8,128)S(1)} %limited_step.1) | data formatting | bytes 65536

commit v10 on v9

--- a/solution.py
+++ b/solution.py
@@ -324,18 +324,21 @@
         for k in range(fields)
         for i in range(GLL_NODES)
     ]
-    spread_out = moved_by_table(jnp.concatenate(parts, axis=0), spread[...])
+    table = spread[...]
+    cut = held * GLL_NODES
+    spread_out = [
+        moved_by_table(jnp.concatenate(group, axis=0), table) for group in (parts[:cut], parts[cut:])
+    ]
     pair = 2 * SLOTS
     in_first = lax.broadcasted_iota(jnp.int32, (elements_x, pair), 1) < SLOTS
 
     def joined(first, second, i, j):
-        first, second = (
-            spread_out[
-                (k * GLL_NODES + i) * elements_x : (k * GLL_NODES + i + 1) * elements_x,
-                j // 2 * pair : (j // 2 + 1) * pair,
-            ]
-            for k in (first, second)
-        )
+        def piece(k):
+            values, at = (spread_out[0], k) if k < held else (spread_out[1], k - held)
+            start = (at * GLL_NODES + i) * elements_x
+            return values[start : start + elements_x, j // 2 * pair : (j // 2 + 1) * pair]
+
+        first, second = piece(first), piece(second)
         if j % 2:
             first = rolled(first, SLOTS, 1)
         else:

time: 11.5 us -> 11.5 us (level)
  no operation moved by 1% of the time
where the time goes in v10:
time: 11.5 us; the launch traced here: 11.3 us
  Pallas kernels  10.7 us (93%)
  local copies, waits for them, and re-layouts  0.62 us (5%)
    pallas_call x1, Pallas kernels, shards(): pl.pallas_call(functools.partial(kernel, n, nz, nlev), out_shape=vmem((nl...  10.7 us
    unnamed x1, local copies, waits for them, and re-layouts  0.62 us

profile of v10, /device:TPU:0, one launch (start us, length us, event | category | flops | bytes accessed | tf_op | source)
XLA Modules:
  0.0 11.3 jit_solution(12641404302204137659)
XLA Ops:
  0.0 10.7 %limited_step.1 = f32[2,4,8,128]{3,2,1,0:T(8,128)S(1)} custom-call(f32[1,8,8,128]{3,2,1,0:T(8,128)} %tracer_hbm.1, f32[1,8,128]{2,1,0:T(8,128)} %mass_hbm.1, f32[1,8,128]{2,1,0:T(8,128)} %wind_x_hbm.1, f32[1,8,128]{2,1,0:T(8,128)} %wind_y_hbm.1, f32[2,2]{1,0:T(2,128)} %remap_hbm.1), custom_call_target="tpu_custom_call" | custom-call | tf_op jit(solution)/shard_map/limited_step/pallas_call | solution.py:440
  10.7 0.6 %copy.7 = f32[2,4,8,128]{3,2,1,0:T(8,128)} copy(f32[2,4,8,128]{3,2,1,0:T(8,128)S(1)} %limited_step.1) | data formatting | bytes 65536

commit v11 on v10

--- a/solution.py
+++ b/solution.py
@@ -196,30 +196,14 @@
                 ready, inc=1, device_id=(x, py - 1, lev), device_id_type=MESH
             )
 
-    remap_copy.start()
-    for copy in copies:
-        copy.wait()
-
-    lane = lax.broadcasted_iota(jnp.int32, (nx, halos.shape[2]), 1)
-
-    def halo_tile(group, side):
-        tile = jnp.zeros(lane.shape, jnp.float32)
-        for k in range(fields):
-            piece = tracer_in[group * held + k] if k < held else metric_in[k - held]
-            shift = width * k - (ny - width if side else 0)
-            wanted = (lane >= width * k) & (lane < width * (k + 1))
-            tile = jnp.where(wanted, rolled(piece, shift, 1), tile)
-        return tile
-
-    for group in range(n):
-        halos_out[0, group] = halo_tile(group, 0)
-
     mine = pl.ds(pl.multiple_of(px * nx, nx), nx)
 
     def block_copies(x):
         pieces = (
-            (tracer_in.at[pl.ds(x * held, held)], blocks.at[:held, mine, :]),
-            (metric_in, blocks.at[held:, mine, :]),
+            (tracer_hbm.at[0, pl.ds(x * held, held)], blocks.at[:held, mine, :]),
+            (mass_hbm.at[0], blocks.at[held, mine, :]),
+            (wind_x_hbm.at[0], blocks.at[held + 1, mine, :]),
+            (wind_y_hbm.at[0], blocks.at[held + 2, mine, :]),
         )
         return [
             pltpu.make_async_remote_copy(
@@ -233,6 +217,28 @@
             for source, target in pieces
         ]
 
+    for x in others():
+        for copy in block_copies(x):
+            copy.start()
+
+    remap_copy.start()
+    for copy in copies:
+        copy.wait()
+
+    lane = lax.broadcasted_iota(jnp.int32, (nx, halos.shape[2]), 1)
+
+    def halo_tile(group, side):
+        tile = jnp.zeros(lane.shape, jnp.float32)
+        for k in range(fields):
+            piece = tracer_in[group * held + k] if k < held else metric_in[k - held]
+            shift = width * k - (ny - width if side else 0)
+            wanted = (lane >= width * k) & (lane < width * (k + 1))
+            tile = jnp.where(wanted, rolled(piece, shift, 1), tile)
+        return tile
+
+    for group in range(n):
+        halos_out[0, group] = halo_tile(group, 0)
+
     def halo_copy(x, side):
         return pltpu.make_async_remote_copy(
             src_ref=halos_out.at[side, x],
@@ -249,10 +255,6 @@
     def _():
         for x in everyone:
             halo_copy(x, 0).start()
-
-    for x in others():
-        for copy in block_copies(x):
-            copy.start()
 
     for group in range(n):
         halos_out[1, group] = halo_tile(group, 1)

time: 11.5 us -> 11.5 us (level)
  no operation moved by 1% of the time
where the time goes in v11:
time: 11.5 us; the launch traced here: 11.3 us
  Pallas kernels  10.7 us (93%)
  local copies, waits for them, and re-layouts  0.62 us (5%)
    pallas_call x1, Pallas kernels, shards(): pl.pallas_call(functools.partial(kernel, n, nz, nlev), out_shape=vmem((nl...  10.7 us
    unnamed x1, local copies, waits for them, and re-layouts  0.62 us

profile of v11, /device:TPU:0, one launch (start us, length us, event | category | flops | bytes accessed | tf_op | source)
XLA Modules:
  0.0 11.3 jit_solution(17865082621673689410)
XLA Ops:
  0.0 10.7 %limited_step.1 = f32[2,4,8,128]{3,2,1,0:T(8,128)S(1)} custom-call(f32[1,8,8,128]{3,2,1,0:T(8,128)} %tracer_hbm.1, f32[1,8,128]{2,1,0:T(8,128)} %mass_hbm.1, f32[1,8,128]{2,1,0:T(8,128)} %wind_x_hbm.1, f32[1,8,128]{2,1,0:T(8,128)} %wind_y_hbm.1, f32[2,2]{1,0:T(2,128)} %remap_hbm.1), custom_call_target="tpu_custom_call" | custom-call | tf_op jit(solution)/shard_map/limited_step/pallas_call | solution.py:442
  10.7 0.6 %copy.7 = f32[2,4,8,128]{3,2,1,0:T(8,128)} copy(f32[2,4,8,128]{3,2,1,0:T(8,128)S(1)} %limited_step.1) | data formatting | bytes 65536
